TPU v7x, 32 devices: a whole 2x2x4 slice. The times are simulated.
32 devices in a mesh: dp: 2 (over y), hid: 4 (over x, core), dm: 4 (over z).
Axes of the slice: x: 2, y: 2, z: 4, core: 2. Of those that a mesh axis runs over, the one named last changes fastest.
Arguments:
- tokens: bfloat16 [10240, 768], P(('dp', 'dm'))
- clusters: int32 [10240], P(('dp', 'dm')), may hold values from 0 to 99, as said below
- top_keys: int32 [200, 32], P('dp'), may hold values from 0 to 5119, as said below
- lengths: int32 [4], P('dp'), may hold values from 1024 to 4096, as said below
- qkv_weight: bfloat16 [3, 768, 768], P(None, None, 'hid')
- out_weight: bfloat16 [768, 768], P('hid'), may hold values from -0.21875 to 0.21875
- first_gain: float32 [768], replicated, may hold values from 0.5 to 1.5
- first_bias: float32 [768], replicated, may hold values from -1.5 to 1.5
- second_gain: float32 [768], replicated, may hold values from 0.5 to 1.5
- second_bias: float32 [768], replicated, may hold values from -1.5 to 1.5
- expand_weight: bfloat16 [768, 3072], P(('dp', 'dm'), 'hid'), may hold values from -0.21875 to 0.21875
- shrink_weight: bfloat16 [3072, 768], P('hid', ('dp', 'dm')), may hold values from -0.109375 to 0.109375
- cotangent: bfloat16 [10240, 768], P(('dp', 'dm')), may hold values from -6 to 6
Outputs:
- result: bfloat16 [10240, 768], P(('dp', 'dm'))
- tokens_grad: bfloat16 [10240, 768], P(('dp', 'dm'))
- qkv_grad: float32 [3, 768, 768], P(None, None, 'hid')
- out_grad: float32 [768, 768], P('hid')
- first_gain_grad: float32 [768], replicated
- first_bias_grad: float32 [768], replicated
- second_gain_grad: float32 [768], replicated
- second_bias_grad: float32 [768], replicated
- expand_grad: float32 [768, 3072], P(('dp', 'dm'), 'hid')
- shrink_grad: float32 [3072, 768], P('hid', ('dp', 'dm'))
Inputs may be any that keep to these rules, and one draw needn't show every extreme that they name: Entries 2p and 2p + 1 are the lengths of the two sequences of pack p, laid end to end in that order; they sum to 5120. `clusters`: cluster numbers count within a pack; every cluster of every pack has 32 queries or more, all in one sequence. `top_keys`: row p * 100 + c lists 32 different positions within pack p, all in the sequence of cluster c's queries.
All inputs are finite; a program needn't handle non-finite values.
Results may differ from a plain program's by a relative error of at most 0.015.
Values may be sent and summed in bfloat16 or wider, within the bound.
A program may use at most 256 MiB of HBM per device.

v0:
```python
import jax
import jax.numpy as jnp
from jax import lax
from jax.sharding import PartitionSpec as P

HEAD_DIM = 64
CL = 100
TOPK = 32


EPSILON = 1e-05
NEGATIVE = -1e30
HIGHEST = lax.Precision.HIGHEST


def norm_parts(values):
    centred = values - jnp.mean(values, -1, keepdims=True)
    spread = lax.rsqrt(jnp.mean(centred * centred, -1, keepdims=True) + EPSILON)
    return (centred * spread, spread)


def norm_back(upstream, normed, spread, norm_gain):
    through = upstream * norm_gain
    inner = (
        through
        - jnp.mean(through, -1, keepdims=True)
        - normed * jnp.mean(through * normed, -1, keepdims=True)
    )
    return (spread * inner, jnp.sum(upstream * normed, 0), jnp.sum(upstream, 0))


def shards(
    tokens,
    clusters,
    top_keys,
    lengths,
    qkv_weight,
    out_weight,
    first_gain,
    first_bias,
    second_gain,
    second_bias,
    expand_weight,
    shrink_weight,
    cotangent,
):
    row_count = tokens.shape[0]
    query_parts = lax.axis_size("dm")
    block_index = lax.axis_index("dm")
    pack_size = row_count * query_parts
    group_width = qkv_weight.shape[2]
    head_count = group_width // HEAD_DIM
    score_scale = HEAD_DIM ** (-0.5)
    slot_count = CL * TOPK
    inputs = tokens.astype(jnp.float32)
    normed_one, spread_one = norm_parts(inputs)
    first_normed = (normed_one * first_gain + first_bias).astype(jnp.bfloat16)
    projected = jnp.einsum(
        "rd,kde->kre", first_normed, qkv_weight, preferred_element_type=jnp.float32
    ).astype(jnp.bfloat16)
    queries = projected[0]
    all_keys, all_values = (
        lax.all_gather(projected[1], "dm", axis=0, tiled=True),
        lax.all_gather(projected[2], "dm", axis=0, tiled=True),
    )
    positions = jnp.arange(pack_size, dtype=jnp.int32)
    segment = (positions >= lengths[0]).astype(jnp.int32)
    own_start = block_index * row_count
    member = clusters[:, None] == jnp.arange(CL, dtype=jnp.int32)[None, :]
    member_low = member.astype(jnp.bfloat16)
    member_full = member.astype(jnp.float32)
    partial_sums = jnp.dot(member_low.T, queries, preferred_element_type=jnp.float32)
    member_counts = jnp.sum(member_full, 0)
    centre_sums, centre_counts = (
        lax.psum(partial_sums.astype(jnp.bfloat16), "dm").astype(jnp.float32),
        lax.psum(member_counts.astype(jnp.bfloat16), "dm").astype(jnp.float32),
    )
    centres = (centre_sums / centre_counts[:, None]).astype(jnp.bfloat16)
    centre_segment = segment[top_keys[:, 0]]
    same_sequence = centre_segment[:, None] == segment[None, :]
    slot_rows = top_keys.reshape(-1)
    top_mask = (
        jnp.zeros((CL, pack_size), jnp.float32).at[jnp.arange(CL)[:, None], top_keys].set(1.0)
    )
    outside_low = (1.0 - top_mask).astype(jnp.bfloat16)
    keys_heads = all_keys.reshape(pack_size, head_count, HEAD_DIM)
    values_heads = all_values.reshape(pack_size, head_count, HEAD_DIM)
    centre_heads = centres.reshape(CL, head_count, HEAD_DIM)

    def centre_scores():
        raw_scores = (
            jnp.einsum("che,phe->hcp", centre_heads, keys_heads, preferred_element_type=jnp.float32)
            * score_scale
        )
        return jnp.where(same_sequence[None], raw_scores, NEGATIVE)

    masked = centre_scores()
    centre_top = jnp.max(masked, -1, keepdims=True)
    centre_exp = jnp.exp(masked - centre_top)
    centre_total = jnp.sum(centre_exp, -1, keepdims=True)
    centre_probs = centre_exp / centre_total
    top_mass = jnp.sum(centre_probs * top_mask[None], -1)
    rest_weights = centre_probs.astype(jnp.bfloat16) * outside_low[None]
    rest_part = jnp.einsum(
        "hcp,phe->che", rest_weights, values_heads, preferred_element_type=jnp.float32
    )
    cluster_keys = all_keys[slot_rows].reshape(CL, TOPK, head_count, HEAD_DIM)
    cluster_values = all_values[slot_rows].reshape(CL, TOPK, head_count, HEAD_DIM)
    mass_rows = top_mass.T
    rest_rows = rest_part.reshape(CL, group_width)
    block_rows = 320
    block_count = row_count // block_rows
    query_blocks = queries.reshape(block_count, block_rows, head_count, HEAD_DIM)
    cluster_blocks = clusters.reshape(block_count, block_rows)

    def exact_scores(query_block, cluster_block):
        key_block = cluster_keys[cluster_block]
        value_block = cluster_values[cluster_block]
        raw_scores = (
            jnp.einsum("bhe,bthe->bht", query_block, key_block, preferred_element_type=jnp.float32)
            * score_scale
        )
        return (raw_scores, key_block, value_block)

    def block_lookup(cluster_block):
        chosen = (cluster_block[:, None] == jnp.arange(CL, dtype=jnp.int32)[None, :]).astype(
            jnp.float32
        )
        return (chosen, jnp.dot(chosen, mass_rows, precision=HIGHEST))

    def forward_block(carried):
        query_block, cluster_block = carried
        scores_block, key_block, value_block = exact_scores(query_block, cluster_block)
        block_top = jnp.max(scores_block, -1, keepdims=True)
        block_exp = jnp.exp(scores_block - block_top)
        block_total = jnp.sum(block_exp, -1, keepdims=True)
        block_probs = (block_exp / block_total).astype(jnp.bfloat16)
        exact_out = jnp.einsum(
            "bht,bthe->bhe", block_probs, value_block, preferred_element_type=jnp.float32
        )
        chosen, mass_here = block_lookup(cluster_block)
        rest_here = jnp.dot(chosen, rest_rows, precision=HIGHEST).reshape(
            block_rows, head_count, HEAD_DIM
        )
        mixed = mass_here[:, :, None] * exact_out + rest_here
        return (mixed.reshape(block_rows, group_width).astype(jnp.bfloat16), block_top, block_total)

    attended, block_tops, block_totals = lax.map(forward_block, (query_blocks, cluster_blocks))
    attended = attended.reshape(row_count, group_width)
    head_part = jnp.dot(attended, out_weight, preferred_element_type=jnp.float32)
    attention_sum = lax.psum(head_part.astype(jnp.bfloat16), "hid").astype(jnp.float32)
    middle = inputs + attention_sum
    normed_two, spread_two = norm_parts(middle)
    second_normed = (normed_two * second_gain + second_bias).astype(jnp.bfloat16)
    expand_full, shrink_full = (
        lax.all_gather(expand_weight, ("dp", "dm"), axis=0, tiled=True),
        lax.all_gather(shrink_weight, ("dp", "dm"), axis=1, tiled=True),
    )
    hidden = jnp.dot(second_normed, expand_full, preferred_element_type=jnp.float32)
    activated = jax.nn.gelu(hidden).astype(jnp.bfloat16)
    hidden_part = jnp.dot(activated, shrink_full, preferred_element_type=jnp.float32)
    hidden_sum = lax.psum(hidden_part.astype(jnp.bfloat16), "hid").astype(jnp.float32)
    result = (middle + hidden_sum).astype(jnp.bfloat16)
    upstream = cotangent.astype(jnp.float32)
    activated_grad = jnp.dot(cotangent, shrink_full.T, preferred_element_type=jnp.float32)
    shrink_local = jnp.dot(activated.T, cotangent, preferred_element_type=jnp.float32)
    gelu_value, gelu_pull = jax.vjp(jax.nn.gelu, hidden)
    hidden_grad = gelu_pull(activated_grad)[0].astype(jnp.bfloat16)
    expand_local = jnp.dot(second_normed.T, hidden_grad, preferred_element_type=jnp.float32)
    second_part = jnp.dot(hidden_grad, expand_full.T, preferred_element_type=jnp.float32)
    second_grad = lax.psum(second_part.astype(jnp.bfloat16), "hid").astype(jnp.float32)
    expand_grad, shrink_grad = (
        lax.psum_scatter(expand_local, ("dp", "dm"), scatter_dimension=0, tiled=True),
        lax.psum_scatter(shrink_local, ("dp", "dm"), scatter_dimension=1, tiled=True),
    )
    middle_inner, second_gain_part, second_bias_part = norm_back(
        second_grad, normed_two, spread_two, second_gain
    )
    middle_grad = upstream + middle_inner
    branch_grad = middle_grad.astype(jnp.bfloat16)
    out_grad_part = jnp.dot(attended.T, branch_grad, preferred_element_type=jnp.float32)
    attended_grad = jnp.dot(branch_grad, out_weight.T, preferred_element_type=jnp.float32)
    gradient_blocks = attended_grad.reshape(block_count, block_rows, head_count, HEAD_DIM)

    def backward_block(running, carried):
        key_slots, value_slots, mass_total, rest_total = running
        query_block, cluster_block, gradient_block, block_top, block_total = carried
        scores_block, key_block, value_block = exact_scores(query_block, cluster_block)
        exact_full = jnp.exp(scores_block - block_top) / block_total
        block_probs = exact_full.astype(jnp.bfloat16)
        exact_out = jnp.einsum(
            "bht,bthe->bhe", block_probs, value_block, preferred_element_type=jnp.float32
        )
        chosen, mass_here = block_lookup(cluster_block)
        exact_grad = (mass_here[:, :, None] * gradient_block).astype(jnp.bfloat16)
        mass_part = jnp.sum(exact_out * gradient_block, -1)
        probability_grad = jnp.einsum(
            "bhe,bthe->bht", exact_grad, value_block, preferred_element_type=jnp.float32
        )
        score_grad = (
            exact_full
            * (probability_grad - jnp.sum(exact_full * probability_grad, -1, keepdims=True))
        ).astype(jnp.bfloat16)
        query_part = (
            jnp.einsum("bht,bthe->bhe", score_grad, key_block, preferred_element_type=jnp.float32)
            * score_scale
        )
        key_rows_part = (
            jnp.einsum("bht,bhe->bthe", score_grad, query_block, preferred_element_type=jnp.float32)
            * score_scale
        )
        value_rows_part = jnp.einsum(
            "bht,bhe->bthe", block_probs, exact_grad, preferred_element_type=jnp.float32
        )
        key_slots = key_slots + jax.ops.segment_sum(key_rows_part, cluster_block, num_segments=CL)
        value_slots = value_slots + jax.ops.segment_sum(
            value_rows_part, cluster_block, num_segments=CL
        )
        mass_total = mass_total + jnp.dot(chosen.T, mass_part, precision=HIGHEST)
        rest_total = rest_total + jnp.dot(
            chosen.T, gradient_block.reshape(block_rows, group_width), precision=HIGHEST
        )
        return (
            (key_slots, value_slots, mass_total, rest_total),
            query_part.reshape(block_rows, group_width),
        )

    empty_slots = jnp.zeros((CL, TOPK, head_count, HEAD_DIM), jnp.float32)
    starting = (
        empty_slots,
        empty_slots,
        jnp.zeros((CL, head_count), jnp.float32),
        jnp.zeros((CL, group_width), jnp.float32),
    )
    (key_slots, value_slots, mass_grad, rest_grad), query_exact = lax.scan(
        backward_block,
        starting,
        (query_blocks, cluster_blocks, gradient_blocks, block_tops, block_totals),
    )
    key_slots = key_slots.reshape(slot_count, group_width)
    value_slots = value_slots.reshape(slot_count, group_width)
    query_exact = query_exact.reshape(row_count, group_width)
    mass_grad, rest_grad = (
        lax.psum(mass_grad.astype(jnp.bfloat16), "dm").astype(jnp.float32),
        lax.psum(rest_grad.astype(jnp.bfloat16), "dm").astype(jnp.float32),
    )
    rest_grad_low = rest_grad.reshape(CL, head_count, HEAD_DIM).astype(jnp.bfloat16)
    masked = centre_scores()
    centre_probs = jnp.exp(masked - centre_top) / centre_total
    rest_weights = centre_probs.astype(jnp.bfloat16) * outside_low[None]
    weight_grad = jnp.einsum(
        "che,phe->hcp", rest_grad_low, values_heads, preferred_element_type=jnp.float32
    )
    probability_grad = (
        weight_grad * (1.0 - top_mask)[None] + mass_grad.T[:, :, None] * top_mask[None]
    )
    score_grad = (
        centre_probs
        * (probability_grad - jnp.sum(centre_probs * probability_grad, -1, keepdims=True))
    ).astype(jnp.bfloat16)
    centre_grad = (
        jnp.einsum("hcp,phe->che", score_grad, keys_heads, preferred_element_type=jnp.float32)
        * score_scale
    ).astype(jnp.bfloat16)
    own_scores = lax.dynamic_slice_in_dim(score_grad, own_start, row_count, 2)
    own_weights = lax.dynamic_slice_in_dim(rest_weights, own_start, row_count, 2)
    key_centre = (
        jnp.einsum("hcr,che->rhe", own_scores, centre_heads, preferred_element_type=jnp.float32)
        * score_scale
    )
    value_centre = jnp.einsum(
        "hcr,che->rhe", own_weights, rest_grad_low, preferred_element_type=jnp.float32
    )
    row_counts = jnp.dot(member_full, centre_counts, precision=HIGHEST)
    query_centre = (
        jnp.dot(
            member_low, centre_grad.reshape(CL, group_width), preferred_element_type=jnp.float32
        )
        / row_counts[:, None]
    )
    key_slots, value_slots = (
        lax.psum(key_slots.astype(jnp.bfloat16), "dm").astype(jnp.float32),
        lax.psum(value_slots.astype(jnp.bfloat16), "dm").astype(jnp.float32),
    )
    local_rows = slot_rows - own_start
    inside = (local_rows >= 0) & (local_rows < row_count)
    target = jnp.where(inside, local_rows, row_count)
    key_exact = (
        jnp.zeros((row_count, group_width), jnp.float32).at[target].add(key_slots, mode="drop")
    )
    value_exact = (
        jnp.zeros((row_count, group_width), jnp.float32).at[target].add(value_slots, mode="drop")
    )
    query_total = (query_exact + query_centre).astype(jnp.bfloat16)
    key_total = (key_exact + key_centre.reshape(row_count, group_width)).astype(jnp.bfloat16)
    value_total = (value_exact + value_centre.reshape(row_count, group_width)).astype(jnp.bfloat16)
    projected_grad = jnp.stack([query_total, key_total, value_total])
    projection_part = jnp.einsum(
        "rd,kre->kde", first_normed, projected_grad, preferred_element_type=jnp.float32
    )
    first_part = jnp.einsum(
        "kre,kde->rd", projected_grad, qkv_weight, preferred_element_type=jnp.float32
    )
    first_grad = lax.psum(first_part.astype(jnp.bfloat16), "hid").astype(jnp.float32)
    inputs_inner, first_gain_part, first_bias_part = norm_back(
        first_grad, normed_one, spread_one, first_gain
    )
    tokens_grad = (middle_grad + inputs_inner).astype(jnp.bfloat16)
    qkv_grad, out_grad, first_gain_grad, first_bias_grad, second_gain_grad, second_bias_grad = (
        lax.psum(
            (
                projection_part,
                out_grad_part,
                first_gain_part,
                first_bias_part,
                second_gain_part,
                second_bias_part,
            ),
            ("dp", "dm"),
        )
    )
    return (
        result,
        tokens_grad,
        qkv_grad,
        out_grad,
        first_gain_grad,
        first_bias_grad,
        second_gain_grad,
        second_bias_grad,
        expand_grad,
        shrink_grad,
    )


def solution(mesh):
    in_specs = (
        P(("dp", "dm"), None),
        P(("dp", "dm")),
        P("dp", None),
        P("dp"),
        P(None, None, "hid"),
        P("hid", None),
        P(),
        P(),
        P(),
        P(),
        P(("dp", "dm"), "hid"),
        P("hid", ("dp", "dm")),
        P(("dp", "dm"), None),
    )
    out_specs = (
        P(("dp", "dm"), None),
        P(("dp", "dm"), None),
        P(None, None, "hid"),
        P("hid", None),
        P(),
        P(),
        P(),
        P(),
        P(("dp", "dm"), "hid"),
        P("hid", ("dp", "dm")),
    )
    return jax.shard_map(shards, mesh=mesh, in_specs=in_specs, out_specs=out_specs, check_vma=False)
```

profile of v0, /device:TPU:0, one launch (start us, length us, event | category | flops | bytes accessed | tf_op | source)
XLA Modules:
  0.0 1984.0 jit_solution(17460848644429064397)
XLA Ops:
  21.7 17.3 scatter_custom_fusion.4
  41.7 23.3 %all-reduce.3 = (bf16[100,192]{0,1:T(8,128)(2,1)S(1)}, bf16[100]{0:T(256)(128)(2,1)S(1)}) all-reduce(bf16[100,192]{0,1:T(8,128)(2,1)S(1)} %convolution_convert_fusion.3, bf16[100]{0:T(256)(128)(2,1)S(1)} %convert_reduce_fusion.3), channel_id=1, replica_groups=mesh['dp'=2,'hid'=4,'dm'=4] {'dm'}, use_global_device_ids=true, to_apply=%region_2.0 | all-reduce | flops 19300 | bytes 77200 | tf_op jit(solution)/shard_map/psum | solution.py:75
  79.1 10.6 gather_fusion.5
  96.7 12.0 all-gather.13.cloned.1.call-done
  113.0 10.6 gather_fusion.6
  142.5 279.8 %while.33 = (s32[]{:T(128)}, bf16[4,320,192]{1,2,0:T(8,128)(2,1)}, f32[4,320,3,1]{1,2,3,0:T(4,128)}, f32[4,320,3,1]{1,2,3,0:T(4,128)}, s32[4,320]{1,0:T(4,128)S(...) while((s32[]{:T(128)}, bf16[4,320,192]{1,2,0:T(8,128)(2,1)}, ...), condition=%wide.region_12.13_spmd, body=%wide.region_9.12_spmd.sunk | while | flops 85204544 | bytes 27198776 | solution.py:148
  147.0 17.5 gather_fusion.1
  164.5 17.4 gather_fusion
  195.9 14.1 multiply_reduce_fusion.6
  216.8 17.5 gather_fusion.1
  234.3 17.4 gather_fusion
  265.7 14.1 multiply_reduce_fusion.6
  286.7 17.5 gather_fusion.1
  304.2 17.4 gather_fusion
  335.5 14.1 multiply_reduce_fusion.6
  356.5 17.5 gather_fusion.1
  374.0 17.4 gather_fusion
  405.3 14.1 multiply_reduce_fusion.6
  435.5 42.1 %all-reduce.12.cloned.1.call-done = bf16[1280,768]{1,0:T(8,128)(2,1)} async-done(((bf16[1280,768]{1,0:T(8,128)(2,1)}), bf16[1280,768]{1,0:T(8,128)(2,1)}) %all-reduce.12.cloned.1.call-update) | async-done | bytes 1966096 | tf_op jit(solution)/shard_map/psum | solution.py:151
  480.9 39.8 %all-gather.7.cloned.1.call-done = bf16[768,768]{1,0:T(8,128)(2,1)} async-done(((bf16[96,768]{1,0:T(8,128)(2,1)}), bf16[768,768]{1,0:T(8,128)(2,1)}) %all-gather.7.cloned.1.call-update) | async-done | bytes 1179664 | tf_op jit(solution)/shard_map/all_gather | solution.py:156
  540.1 41.1 %all-reduce.14.cloned.1.call-done = bf16[1280,768]{1,0:T(8,128)(2,1)} async-done(((bf16[1280,768]{1,0:T(8,128)(2,1)}), bf16[1280,768]{1,0:T(8,128)(2,1)}) %all-reduce.14.cloned.1.call-update) | async-done | bytes 1966096 | tf_op jit(solution)/shard_map/psum | solution.py:171
  598.8 816.3 %while.34 = (s32[]{:T(128)}, f32[100,32,3,64]{3,1,2,0:T(8,128)}, f32[100,32,3,64]{3,1,2,0:T(8,128)}, f32[100,3]{0,1:T(4,128)S(1)}, f32[100,192]{0,1:T(8,128)S(1)...) while((s32[]{:T(128)}, f32[100,32,3,64]{3,1,2,0:T(8,128)}, ...), condition=%wide.region_25.26_spmd.clone, body=%wide.region_20.25_spmd.clone.sunk | while | flops 102496056 | bytes 119429096 | solution.py:235
  604.0 17.4 gather_fusion.3
  621.4 17.5 gather_fusion.2
  683.6 56.5 %scatter_fusion.1 = f32[100,32,3,64]{3,1,2,0:T(8,128)} fusion(f32[100,32,3,64]{3,1,2,0:T(8,128)} %get-tuple-element.636, s32[320]{0:T(512)S(1)} %fusion.216, f32[320,32,3,64]{3,1,2,0:T(8,128)} %multiply_bitcast_fusion.5), kind=kCustom, calls=%fused_computation.8.clone.clone.1 | custom fusion | flops 1966080 | bytes 23594240 | tf_op jit(solution)/shard_map/while/body/eval_jaxpr/scatter-add | solution.py:216
  746.1 56.6 %scatter_fusion = f32[100,32,3,64]{3,1,2,0:T(8,128)} fusion(f32[100,32,3,64]{3,1,2,0:T(8,128)} %get-tuple-element.635, s32[320]{0:T(512)S(1)} %fusion.216, f32[320,32,3,64]{3,1,2,0:T(8,128)} %multiply_bitcast_fusion.4), kind=kCustom, calls=%fused_computation.7.clone.clone.1 | custom fusion | flops 1966080 | bytes 23594240 | tf_op jit(solution)/shard_map/while/body/eval_jaxpr/scatter-add | solution.py:215
  807.8 17.4 gather_fusion.3
  825.2 17.5 gather_fusion.2
  887.4 56.7 %scatter_fusion.1 = f32[100,32,3,64]{3,1,2,0:T(8,128)} fusion(f32[100,32,3,64]{3,1,2,0:T(8,128)} %get-tuple-element.636, s32[320]{0:T(512)S(1)} %fusion.216, f32[320,32,3,64]{3,1,2,0:T(8,128)} %multiply_bitcast_fusion.5), kind=kCustom, calls=%fused_computation.8.clone.clone.1 | custom fusion | flops 1966080 | bytes 23594240 | tf_op jit(solution)/shard_map/while/body/eval_jaxpr/scatter-add | solution.py:216
  950.1 56.8 %scatter_fusion = f32[100,32,3,64]{3,1,2,0:T(8,128)} fusion(f32[100,32,3,64]{3,1,2,0:T(8,128)} %get-tuple-element.635, s32[320]{0:T(512)S(1)} %fusion.216, f32[320,32,3,64]{3,1,2,0:T(8,128)} %multiply_bitcast_fusion.4), kind=kCustom, calls=%fused_computation.7.clone.clone.1 | custom fusion | flops 1966080 | bytes 23594240 | tf_op jit(solution)/shard_map/while/body/eval_jaxpr/scatter-add | solution.py:215
  1011.9 17.4 gather_fusion.3
  1029.3 17.5 gather_fusion.2
  1091.5 56.5 %scatter_fusion.1 = f32[100,32,3,64]{3,1,2,0:T(8,128)} fusion(f32[100,32,3,64]{3,1,2,0:T(8,128)} %get-tuple-element.636, s32[320]{0:T(512)S(1)} %fusion.216, f32[320,32,3,64]{3,1,2,0:T(8,128)} %multiply_bitcast_fusion.5), kind=kCustom, calls=%fused_computation.8.clone.clone.1 | custom fusion | flops 1966080 | bytes 23594240 | tf_op jit(solution)/shard_map/while/body/eval_jaxpr/scatter-add | solution.py:216
  1154.1 56.7 %scatter_fusion = f32[100,32,3,64]{3,1,2,0:T(8,128)} fusion(f32[100,32,3,64]{3,1,2,0:T(8,128)} %get-tuple-element.635, s32[320]{0:T(512)S(1)} %fusion.216, f32[320,32,3,64]{3,1,2,0:T(8,128)} %multiply_bitcast_fusion.4), kind=kCustom, calls=%fused_computation.7.clone.clone.1 | custom fusion | flops 1966080 | bytes 23594240 | tf_op jit(solution)/shard_map/while/body/eval_jaxpr/scatter-add | solution.py:215
  1215.8 17.4 gather_fusion.3
  1233.2 17.5 gather_fusion.2
  1295.4 56.6 %scatter_fusion.1 = f32[100,32,3,64]{3,1,2,0:T(8,128)} fusion(f32[100,32,3,64]{3,1,2,0:T(8,128)} %get-tuple-element.636, s32[320]{0:T(512)S(1)} %fusion.216, f32[320,32,3,64]{3,1,2,0:T(8,128)} %multiply_bitcast_fusion.5), kind=kCustom, calls=%fused_computation.8.clone.clone.1 | custom fusion | flops 1966080 | bytes 23594240 | tf_op jit(solution)/shard_map/while/body/eval_jaxpr/scatter-add | solution.py:216
  1358.0 56.7 %scatter_fusion = f32[100,32,3,64]{3,1,2,0:T(8,128)} fusion(f32[100,32,3,64]{3,1,2,0:T(8,128)} %get-tuple-element.635, s32[320]{0:T(512)S(1)} %fusion.216, f32[320,32,3,64]{3,1,2,0:T(8,128)} %multiply_bitcast_fusion.4), kind=kCustom, calls=%fused_computation.7.clone.clone.1 | custom fusion | flops 1966080 | bytes 23594240 | tf_op jit(solution)/shard_map/while/body/eval_jaxpr/scatter-add | solution.py:215
  1418.1 17.3 all-reduce.2
  1464.2 9.3 multiply_reduce_fusion.1
  1493.6 93.7 %all-reduce.18.cloned.1.call-done = (bf16[3200,192]{1,0:T(8,128)(2,1)}, bf16[3200,192]{1,0:T(8,128)(2,1)}) async-done(((bf16[3200,192]{1,0:T(8,128)(2,1)}, bf16[3200,192]{1,0:T(8,128)(2,1)}), (bf16[3200,192]{1,0:T(8,128)(2,1)}, bf16[3200,192]{1,0:T(8,128)(2,1)})) %all-reduce.18.cloned.1.call-update) | async-done | bytes 2457616 | tf_op jit(solution)/shard_map/psum | solution.py:283
  1587.3 20.8 %scatter_custom_fusion.2 = f32[1280,192]{1,0:T(8,128)} fusion(f32[1280,192]{1,0:T(8,128)} %copy.114, s32[3200]{0:T(1024)} %get-tuple-element.321, bf16[3200,192]{1,0:T(8,128)(2,1)} %get-tuple-element.382), kind=kCustom, calls=%fused_computation.150 | custom fusion | flops 1228800 | bytes 2621440 | tf_op jit(solution)/shard_map/scatter-add | solution.py:289
  1609.7 20.1 %scatter_custom_fusion.3 = f32[1280,192]{1,0:T(8,128)S(1)} fusion(f32[1280,192]{1,0:T(8,128)S(1)} %copy-done.17, s32[3200]{0:T(1024)} %get-tuple-element.321, bf16[3200,192]{1,0:T(8,128)(2,1)} %get-tuple-element.381), kind=kCustom, calls=%fused_computation.148 | custom fusion | flops 1228800 | bytes 2621440 | tf_op jit(solution)/shard_map/scatter-add | solution.py:292
  1655.0 60.4 %all-reduce.20.cloned.1.call-done = (bf16[1280,768]{1,0:T(8,128)(2,1)}, bf16[1280,768]{1,0:T(8,128)(2,1)}) async-done(((bf16[1280,768]{1,0:T(8,128)(2,1)}, bf16[1280,768]{1,0:T(8,128)(2,1)}), (bf16[1280,768]{1,0:T(8,128)(2,1)}, bf16[1280,768]{1,0:T(8,128)(2,1)})) %all-reduce.20.cloned.1.call-update) | async-done | bytes 3932176 | tf_op jit(solution)/shard_map/psum | solution.py:162
  1718.8 38.3 %all-reduce = (f32[768]{0:T(1024)}, f32[768]{0:T(1024)}, f32[768]{0:T(1024)}, f32[768]{0:T(1024)}) all-reduce(f32[768]{0:T(1024)S(1)} %get-tuple-element.315, f32[768]{0:T(1024)S(1)} %get-tuple-element.320, f32[768]{0:T(1024)S(1)} %copy-done.49, f32[768]{0:T(1024)S(1)} %copy-done.50), channel_id=1, replica_groups=mesh['dp'=2,'hid'=4,'dm'=4] {'dp','dm'}, use_global_device_ids=true, to_apply=%region_39.40 | all-reduce | flops 3072 | bytes 24576 | tf_op jit(solution)/shard_map/psum | solution.py:310
  1763.2 25.9 %reduce-scatter.3.cloned.1.call-done = f32[96,768]{1,0:T(8,128)} async-done(((f32[768,768]{1,0:T(8,128)}), f32[96,768]{1,0:T(8,128)}) %reduce-scatter.3.cloned.1.call-update) | async-done | bytes 294928 | tf_op jit(solution)/shard_map/reduce_scatter | solution.py:173
  1789.1 72.1 %reduce-scatter.5.cloned.1.call-done = f32[768,96]{0,1:T(8,128)} async-done(((f32[768,768]{0,1:T(8,128)}), f32[768,96]{0,1:T(8,128)}) %reduce-scatter.5.cloned.1.call-update) | async-done | bytes 294928 | tf_op jit(solution)/shard_map/reduce_scatter | solution.py:174
  1861.3 112.3 %all-reduce.16.cloned.1.call-done = (f32[3,768,192]{1,2,0:T(8,128)}, f32[192,768]{1,0:T(8,128)}) async-done(((f32[3,768,192]{1,2,0:T(8,128)}, f32[192,768]{1,0:T(8,128)}), (f32[3,768,192]{1,2,0:T(8,128)}, f32[192,768]{1,0:T(8,128)})) %all-reduce.16.cloned.1.call-update) | async-done | bytes 2359312 | tf_op jit(solution)/shard_map/psum | solution.py:310
  (459 shorter events, 511.6 us)
Async XLA Ops:
  7.2 67.6 %all-gather.11.cloned.1.call-start = ((), (), s32[]{:S(2)}) async-start(), calls=%async_computation.8 | async-start | bytes 2457600 | tf_op jit(solution)/shard_map/all_gather | solution.py:63
  13.2 5.8 copy-start.54
  13.2 5.9 copy-start.56
  15.7 93.0 %all-gather.13.cloned.1.call-start = ((), (), s32[]{:S(2)}) async-start(), calls=%async_computation.9 | async-start | bytes 2457600 | tf_op jit(solution)/shard_map/all_gather | solution.py:64
  16.4 413.6 %all-gather.9.cloned.1.call-start = ((), (), s32[]{:S(2)}) async-start(), calls=%async_computation.4 | async-start | bytes 1327104 | tf_op jit(solution)/shard_map/all_gather | solution.py:157
  17.2 460.5 %all-reduce.12.cloned.1.call-start = ((), (), s32[]{:S(2)}) async-start(), calls=%async_computation.2 | async-start | bytes 3932160 | tf_op jit(solution)/shard_map/psum | solution.py:151
  65.0 9.8 copy-start.62
  74.8 55.7 %copy-start.25 = (bf16[100,192]{0,1:T(8,128)(2,1)}, bf16[100,192]{0,1:T(8,128)(2,1)S(1)}, u32[]{:S(2)}) copy-start(bf16[100,192]{0,1:T(8,128)(2,1)S(1)} %divide_convert_fusion.1) | copy-start | bytes 115204
  422.3 13.2 copy-start.51
  426.2 9.3 copy-start.18
  429.4 91.4 %all-gather.7.cloned.1.call-start = ((), (), s32[]{:S(2)}) async-start(), calls=%async_computation.3 | async-start | bytes 1327104 | tf_op jit(solution)/shard_map/all_gather | solution.py:156
  430.0 151.2 %all-reduce.14.cloned.1.call-start = ((), (), s32[]{:S(2)}) async-start(), calls=%async_computation.5 | async-start | bytes 3932160 | tf_op jit(solution)/shard_map/psum | solution.py:171
  435.5 85.2 %copy-start.45 = (f32[768]{0:T(1024)S(1)}, f32[768]{0:T(1024)}, u32[]{:S(2)}) copy-start(f32[768]{0:T(1024)} %param.25) | copy-start | bytes 9220
  435.5 85.2 %copy-start.58 = (f32[768]{0:T(1024)S(1)}, f32[768]{0:T(1024)}, u32[]{:S(2)}) copy-start(f32[768]{0:T(1024)} %param.26) | copy-start | bytes 9220
  479.9 106.5 %copy-start.33 = (f32[1280]{0:T(1024)}, f32[1280]{0:T(1024)S(1)}, u32[]{:S(2)}) copy-start(f32[1280]{0:T(1024)S(1)} %broadcast_multiply_fusion.4) | copy-start | bytes 15364
  480.9 105.5 %copy-start.37 = (f32[1280]{0:T(1024)}, f32[1280]{0:T(1024)S(1)}, u32[]{:S(2)}) copy-start(f32[1280]{0:T(1024)S(1)} %add_rsqrt_fusion) | copy-start | bytes 15364
  520.8 9.3 copy-start.57
  533.1 1054.3 %all-reduce.18.cloned.1.call-start = ((), (), s32[]{:S(2)}) async-start(), calls=%async_computation.11 | async-start | bytes 6553600 | tf_op jit(solution)/shard_map/psum | solution.py:283
  593.0 5.7 copy-start.52
  638.9 9.2 copy-start.1
  683.6 56.5 %copy-start.5 = (f32[320,3,32]{2,1,0:T(4,128)S(1)}, f32[320,3,32]{2,1,0:T(4,128)}, u32[]{:S(2)}) copy-start(f32[320,3,32]{2,1,0:T(4,128)} %get-tuple-element.580) | copy-start | bytes 368644 | tf_op jit(solution)/shard_map/while
  746.1 56.6 %copy-start.53 = (f32[100,3]{0,1:T(4,128)S(1)}, f32[100,3]{0,1:T(4,128)}, u32[]{:S(2)}) copy-start(f32[100,3]{0,1:T(4,128)} %get-tuple-element.755) | copy-start | bytes 3604 | tf_op jit(solution)/shard_map/while
  842.7 9.2 copy-start.1
  887.4 56.7 %copy-start.5 = (f32[320,3,32]{2,1,0:T(4,128)S(1)}, f32[320,3,32]{2,1,0:T(4,128)}, u32[]{:S(2)}) copy-start(f32[320,3,32]{2,1,0:T(4,128)} %get-tuple-element.580) | copy-start | bytes 368644 | tf_op jit(solution)/shard_map/while
  950.1 56.8 %copy-start.53 = (f32[100,3]{0,1:T(4,128)S(1)}, f32[100,3]{0,1:T(4,128)}, u32[]{:S(2)}) copy-start(f32[100,3]{0,1:T(4,128)} %get-tuple-element.755) | copy-start | bytes 3604 | tf_op jit(solution)/shard_map/while
  1046.8 9.2 copy-start.1
  1091.5 56.6 %copy-start.5 = (f32[320,3,32]{2,1,0:T(4,128)S(1)}, f32[320,3,32]{2,1,0:T(4,128)}, u32[]{:S(2)}) copy-start(f32[320,3,32]{2,1,0:T(4,128)} %get-tuple-element.580) | copy-start | bytes 368644 | tf_op jit(solution)/shard_map/while
  1154.1 56.7 %copy-start.53 = (f32[100,3]{0,1:T(4,128)S(1)}, f32[100,3]{0,1:T(4,128)}, u32[]{:S(2)}) copy-start(f32[100,3]{0,1:T(4,128)} %get-tuple-element.755) | copy-start | bytes 3604 | tf_op jit(solution)/shard_map/while
  1250.7 9.2 copy-start.1
  1295.4 56.6 %copy-start.5 = (f32[320,3,32]{2,1,0:T(4,128)S(1)}, f32[320,3,32]{2,1,0:T(4,128)}, u32[]{:S(2)}) copy-start(f32[320,3,32]{2,1,0:T(4,128)} %get-tuple-element.580) | copy-start | bytes 368644 | tf_op jit(solution)/shard_map/while
  1358.0 56.7 %copy-start.53 = (f32[100,3]{0,1:T(4,128)S(1)}, f32[100,3]{0,1:T(4,128)}, u32[]{:S(2)}) copy-start(f32[100,3]{0,1:T(4,128)} %get-tuple-element.755) | copy-start | bytes 3604 | tf_op jit(solution)/shard_map/while
  1456.9 7.3 copy-start.11
  1456.9 7.3 copy-start.44
  1464.0 251.5 %all-reduce.20.cloned.1.call-start = ((), (), s32[]{:S(2)}) async-start(), calls=%async_computation.12 | async-start | bytes 7864320 | tf_op jit(solution)/shard_map/psum | solution.py:162
  1464.2 9.4 slice-start
  1464.2 9.4 slice-start.1
  1473.6 6.5 copy-start.26
  1480.1 9.0 copy-start.9
  1486.4 6.0 copy-start.42
  1486.4 6.0 copy-start.64
  1492.5 117.2 %copy-start.17 = (f32[1280,192]{1,0:T(8,128)S(1)}, f32[1280,192]{1,0:T(8,128)}, u32[]{:S(2)}) copy-start(f32[1280,192]{1,0:T(8,128)} %copy.117) | copy-start | bytes 2949124
  1609.7 20.4 %copy-start.27 = (bf16[1280,192]{0,1:T(8,128)(2,1)}, bf16[1280,192]{0,1:T(8,128)(2,1)S(1)}, u32[]{:S(2)}) copy-start(bf16[1280,192]{0,1:T(8,128)(2,1)S(1)} %copy.115) | copy-start | bytes 1474564
  1634.9 154.3 %reduce-scatter.3.cloned.1.call-start = ((), (), s32[]{:S(2)}) async-start(), calls=%async_computation.6 | async-start | bytes 2654208 | tf_op jit(solution)/shard_map/reduce_scatter | solution.py:173
  1642.1 6.4 copy-start.19
  1642.1 219.2 %reduce-scatter.5.cloned.1.call-start = ((), (), s32[]{:S(2)}) async-start(), calls=%async_computation.7 | async-start | bytes 2654208 | tf_op jit(solution)/shard_map/reduce_scatter | solution.py:174
  1648.5 325.1 %all-reduce.16.cloned.1.call-start = ((), (), s32[]{:S(2)}) async-start(), calls=%async_computation.10 | async-start | bytes 4718592 | tf_op jit(solution)/shard_map/psum | solution.py:310
  1655.0 63.8 %copy-start.49 = (f32[768]{0:T(1024)S(1)}, f32[768]{0:T(1024)}, u32[]{:S(2)}) copy-start(f32[768]{0:T(1024)} %get-tuple-element.313) | copy-start | bytes 9220
  1655.0 63.8 %copy-start.50 = (f32[768]{0:T(1024)S(1)}, f32[768]{0:T(1024)}, u32[]{:S(2)}) copy-start(f32[768]{0:T(1024)} %get-tuple-element.319) | copy-start | bytes 9220
  (41 other events, 126.0 us)
Sparse Core Ops, SparseCore 0:
  15.8 48.2 all-gather.10
  66.3 42.4 all-gather.12
  110.8 39.8 all-gather.8
  429.5 48.0 all-reduce.11
  479.6 41.1 all-gather.6
  533.2 47.9 all-reduce.13
  1464.1 123.1 all-reduce.17
  1635.0 80.4 all-reduce.19
  1719.5 69.5 reduce-scatter.2
  1793.1 68.1 reduce-scatter.4
  1865.4 108.0 all-reduce.15
where the time goes:
time: 2000 us; the launch traced here: 1980 us
  other arithmetic  664 us (33%)
  waiting for transfers between devices  502 us (25%)
  local copies, waits for them, and re-layouts  500 us (25%)
  matrix products  222 us (11%)
  blocking collectives  78.9 us (4%)
    scatter-add x4, other arithmetic, backward_block(): jax.ops.segment_sum(key_rows_part, cluster_block, num_segments=CL)  227 us
    scatter-add x4, other arithmetic, backward_block(): jax.ops.segment_sum(value_rows_part, cluster_block, num_segments=CL)  226 us
    gather x8, local copies, waits for them, and re-layouts, exact_scores(): value_block = cluster_values[cluster_block]  139 us
    gather x8, local copies, waits for them, and re-layouts, exact_scores(): key_block = cluster_keys[cluster_block]  139 us
    psum x1, waiting for transfers between devices, shards(): lax.psum((projection_part, out_grad_part, first_gain_part, first_bias_par...  112 us
    psum x1, waiting for transfers between devices, shards(): lax.psum(value_slots.astype(jnp.bfloat16), 'dm').astype(jnp.float32)  93.7 us
    reduce_scatter x1, waiting for transfers between devices, shards(): lax.psum_scatter(shrink_local, ('dp', 'dm'), scatter_dimension=1, tiled=T...  72.1 us
    dot_general x8, matrix products, exact_scores(): jnp.einsum('bhe,bthe->bht', query_block, key_block, preferred_element_typ...  66.2 us
  transfers between devices with their start and end apart: 11, of which 9 were waited for; matrix products, arithmetic and copies ran while one was open for 22% of the time, Pallas kernels for 0%

commit v1 on v0

v1 whole, which is shorter than its diff:
```python
import functools

import jax
import jax.numpy as jnp
from jax import lax
from jax.experimental import pallas as pl
from jax.experimental.pallas import tpu as pltpu
from jax.sharding import PartitionSpec as P

HEAD_DIM = 64
CL = 100
TOPK = 32
CLP = 128
SLOTS = 3328
GROUP = 8
GSLOTS = GROUP * TOPK
GROUPS = SLOTS // GSLOTS
WIN = 128
EPSILON = 1e-05
NEGATIVE = -1e30
HIGHEST = lax.Precision.HIGHEST
F32 = jnp.float32
BF16 = jnp.bfloat16
MESH = pl.DeviceIdType.MESH
NT = (((1,), (1,)), ((), ()))
TN = (((0,), (0,)), ((), ()))
SCALE = HEAD_DIM ** (-0.5)


def dot(a, b):
    return jnp.dot(a, b, preferred_element_type=F32)


def dot_nt(a, b):
    return lax.dot_general(a, b, NT, preferred_element_type=F32)


def dot_tn(a, b):
    return lax.dot_general(a, b, TN, preferred_element_type=F32)


def iota(shape, dim):
    return lax.broadcasted_iota(jnp.int32, shape, dim)


def norm_parts(values):
    centred = values - jnp.mean(values, -1, keepdims=True)
    spread = lax.rsqrt(jnp.mean(centred * centred, -1, keepdims=True) + EPSILON)
    return (centred * spread, spread)


def norm_back(upstream, normed, spread, norm_gain):
    through = upstream * norm_gain
    inner = (
        through
        - jnp.mean(through, -1, keepdims=True)
        - normed * jnp.mean(through * normed, -1, keepdims=True)
    )
    return (spread * inner, jnp.sum(upstream * normed, 0), jnp.sum(upstream, 0))


def head_lanes(width, head):
    lane = iota((1, width), 1)
    return lane // HEAD_DIM == head


def block_diagonal(rows, heads):
    width = rows.shape[1]
    zero = jnp.zeros_like(rows)
    return jnp.concatenate(
        [jnp.where(head_lanes(width, h), rows, zero) for h in range(heads)], axis=0
    )


def diagonal_blocks(full, heads):
    rows, width = full.shape[0] // heads, full.shape[1]
    out = full[:rows]
    for h in range(1, heads):
        out = jnp.where(head_lanes(width, h), full[h * rows : (h + 1) * rows], out)
    return out


def front_kernel(
    tok, ccol, crow, weight, gain, bias,
    fn_out, qs_out, k_out, v_out, csum_out, starts_out, rcol_out, rrow_out, cls_out,
    q_ref, member_ref,
):
    rows = tok.shape[0]
    width = weight.shape[2]
    tiles = rows // 128
    lower = (iota((128, 128), 0) > iota((128, 128), 1)).astype(BF16)
    lane = iota((128, 128), 1)
    csum_out[...] = jnp.zeros_like(csum_out)

    def tile(i, running):
        at = pl.ds(pl.multiple_of(i * 128, 128), 128)
        normed, _ = norm_parts(tok[at, :].astype(F32))
        first = (normed * gain[...] + bias[...]).astype(BF16)
        fn_out[at, :] = first
        q = dot(first, weight[0]).astype(BF16)
        q_ref[at, :] = q
        k_out[at, :] = dot(first, weight[1]).astype(BF16)
        v_out[at, :] = dot(first, weight[2]).astype(BF16)
        member = (ccol[at, :] == lane).astype(F32)
        low = member.astype(BF16)
        member_ref[at, :] = low
        extended = jnp.concatenate([q, jnp.ones((128, 256 - width), BF16)], axis=1)
        csum_out[...] += dot_tn(low, extended)
        earlier = dot(lower, low) + running
        rcol_out[at, :] = jnp.sum(member * earlier, 1, keepdims=True)
        return running + jnp.sum(member, 0, keepdims=True)

    counts = lax.fori_loop(0, tiles, tile, jnp.zeros((1, 128), F32))
    before = (iota((128, 128), 0) < iota((128, 128), 1)).astype(F32)
    starts = jnp.dot(
        jnp.broadcast_to(counts, (8, 128)), before, precision=HIGHEST, preferred_element_type=F32
    )
    starts_out[...] = starts.astype(jnp.int32)

    def ranks(i, carry):
        at = pl.ds(pl.multiple_of(i * 128, 128), 128)
        member = member_ref[at, :].astype(F32)
        rank = rcol_out[at, :] + jnp.sum(member * starts[:1], 1, keepdims=True)
        rcol_out[at, :] = rank
        turned = jnp.transpose(jnp.broadcast_to(rank, (128, 128)))
        rrow_out[:, at] = turned[:8]
        return carry

    lax.fori_loop(0, tiles, ranks, 0)
    rank_row = rrow_out[:1, :].astype(jnp.int32)

    def place(i, carry):
        at = pl.ds(pl.multiple_of(i * 128, 128), 128)
        chosen = (iota((128, rows), 0) + i * 128 == rank_row).astype(BF16)
        qs_out[at, :] = dot(chosen, q_ref[...]).astype(BF16)
        sorted_member = dot(chosen, member_ref[...])
        cls_out[at, :] = jnp.sum(sorted_member * lane.astype(F32), 1, keepdims=True).astype(
            jnp.int32
        )
        return carry

    lax.fori_loop(0, tiles, place, 0)
    qs_out[rows:, :] = jnp.zeros((WIN, width), BF16)
    cls_out[rows:, :] = jnp.full((WIN, 1), -1, jnp.int32)


def vmem(n):
    return [pl.BlockSpec(memory_space=pltpu.VMEM)] * n


def front(tokens, clusters, qkv_weight, gain, bias):
    rows = tokens.shape[0]
    width = qkv_weight.shape[2]
    shape = jax.ShapeDtypeStruct
    return pl.pallas_call(
        front_kernel,
        out_shape=(
            shape(tokens.shape, BF16),
            shape((rows + WIN, width), BF16),
            shape((rows, width), BF16),
            shape((rows, width), BF16),
            shape((CLP, 256), F32),
            shape((8, 128), jnp.int32),
            shape((rows, 1), F32),
            shape((8, rows), F32),
            shape((rows + WIN, 1), jnp.int32),
        ),
        in_specs=vmem(6),
        out_specs=tuple(vmem(9)),
        scratch_shapes=[pltpu.VMEM((rows, width), BF16), pltpu.VMEM((rows, 128), BF16)],
        compiler_params=pltpu.CompilerParams(vmem_limit_bytes=40 << 20),
        name="front",
    )(tokens, clusters.reshape(rows, 1), clusters.reshape(1, rows), qkv_weight, gain[None], bias[None])


def sequence_masks(lengths, topk, rows):
    own_start = lax.axis_index("dm") * rows
    key_second = iota((1, rows), 1) + own_start >= lengths[0]
    centre_second = topk[:, :1] >= lengths[0]
    return key_second == centre_second


def centre_forward_kernel(lengths, csum, k, v, topk, centre_out, tm_out, stat_out):
    rows, width = k.shape
    heads = width // HEAD_DIM
    own_start = lax.axis_index("dm") * rows
    count = jnp.maximum(csum[:, width : width + 1], 1.0)
    centre = (csum[:, :width] / count).astype(BF16)
    centre_out[...] = centre
    here = iota((CLP, rows), 1) + own_start
    hit = topk[:, :1] == here
    for t in range(1, TOPK):
        hit = hit | (topk[:, t : t + 1] == here)
    top = hit.astype(F32)
    tm_out[...] = top.astype(BF16)
    outside = 1.0 - top
    same = sequence_masks(lengths, topk, rows)
    full = dot_nt(block_diagonal(centre, heads), k[...]) * SCALE
    lane = iota((CLP, 128), 1)
    stats = jnp.zeros((CLP, 128), F32)
    weights = []
    for h in range(heads):
        scores = jnp.where(same, full[h * CLP : (h + 1) * CLP], NEGATIVE)
        largest = jnp.max(scores, 1, keepdims=True)
        raised = jnp.exp(scores - largest)
        total = jnp.sum(raised, 1, keepdims=True)
        mass = jnp.sum(raised * top, 1, keepdims=True)
        weights.append((raised * outside).astype(BF16))
        stats = jnp.where(lane == h, largest, stats)
        stats = jnp.where(lane == 8 + h, total, stats)
        stats = jnp.where(lane == 16 + h, mass, stats)
    rest = diagonal_blocks(dot(jnp.concatenate(weights, axis=0), v[...]), heads)
    stat_out[:, :256] = jnp.concatenate([rest, jnp.zeros((CLP, 256 - width), F32)], axis=1)
    stat_out[:, 256:] = stats


def centre_forward(lengths, csum, k, v, topk):
    rows, width = k.shape
    shape = jax.ShapeDtypeStruct
    return pl.pallas_call(
        centre_forward_kernel,
        out_shape=(
            shape((CLP, width), BF16),
            shape((CLP, rows), BF16),
            shape((CLP, 384), F32),
        ),
        in_specs=[pl.BlockSpec(memory_space=pltpu.SMEM)] + vmem(4),
        out_specs=tuple(vmem(3)),
        compiler_params=pltpu.CompilerParams(vmem_limit_bytes=40 << 20),
        name="centre_forward",
    )(lengths, csum, k, v, topk)


def merge_stats(stats, heads, width):
    parts = stats.shape[0]
    largest = stats[0][:, 256:]
    for d in range(1, parts):
        largest = jnp.maximum(largest, stats[d][:, 256:])
    total = jnp.zeros((CLP, 1), F32)
    mass_rows = jnp.zeros((CLP, width), F32)
    rest_rows = jnp.zeros((CLP, width), F32)
    lane = iota((CLP, 128), 1)
    merged = jnp.zeros((CLP, 128), F32)
    for h in range(heads):
        top = largest[:, h : h + 1]
        total = jnp.zeros((CLP, 1), F32)
        mass = jnp.zeros((CLP, 1), F32)
        rest = jnp.zeros((CLP, width), F32)
        for d in range(parts):
            block = stats[d]
            factor = jnp.exp(block[:, 256 + h : 257 + h] - top)
            total += factor * block[:, 264 + h : 265 + h]
            mass += factor * block[:, 272 + h : 273 + h]
            rest += factor * block[:, :width]
        mine = head_lanes(width, h)
        mass = mass / total
        mass_rows = jnp.where(mine, mass, mass_rows)
        rest_rows = jnp.where(mine, rest / total, rest_rows)
        merged = jnp.where(lane == h, top, merged)
        merged = jnp.where(lane == 8 + h, total, merged)
        merged = jnp.where(lane == 16 + h, mass, merged)
    return mass_rows, rest_rows, merged


def exact_forward_kernel(
    starts, qs, cls, ks, vs, stats, rcol, att_out, rows_out, merged_out, att_s, mix_s
):
    rows, width = rcol.shape[0], qs.shape[1]
    heads = width // HEAD_DIM
    tiles = rows // 128
    mass_rows, rest_rows, merged = merge_stats(stats, heads, width)
    rows_out[:, :width] = mass_rows
    rows_out[:, width:] = rest_rows
    merged_out[...] = merged
    both = jnp.concatenate([mass_rows, rest_rows], axis=1)
    high = both.astype(BF16)
    low = (both - high.astype(F32)).astype(BF16)
    lane = iota((128, 128), 1)

    def spread(i, carry):
        at = pl.ds(pl.multiple_of(i * 128, 128), 128)
        member = (cls[at, :] == lane).astype(BF16)
        mix_s[at, :] = dot(member, high) + dot(member, low)
        return carry

    lax.fori_loop(0, tiles + 1, spread, 0)
    slot_cluster = iota((WIN, GSLOTS), 1) // TOPK

    def group(g, carry):
        at = pl.ds(pl.multiple_of(g * GSLOTS, GSLOTS), GSLOTS)
        keys = block_diagonal(ks[at, :], heads)
        values = block_diagonal(vs[at, :], heads)
        first, last = starts[0, g * GROUP], starts[0, g * GROUP + GROUP]
        base = first // 16 * 16
        windows = jnp.where(last > first, (last - base + WIN - 1) // WIN, 0)

        def window(w, carry):
            row = pl.multiple_of(base + w * WIN, 16)
            here = pl.ds(row, WIN)
            mine = cls[here, :] == slot_cluster + g * GROUP
            scores = dot_nt(qs[here, :], keys) * SCALE
            weights = []
            for h in range(heads):
                part = jnp.where(mine, scores[:, h * GSLOTS : (h + 1) * GSLOTS], NEGATIVE)
                raised = jnp.where(mine, jnp.exp(part - jnp.max(part, 1, keepdims=True)), 0.0)
                total = jnp.maximum(jnp.sum(raised, 1, keepdims=True), 0.5)
                weights.append((raised / total).astype(BF16))
            out = dot(jnp.concatenate(weights, axis=1), values)
            mix = mix_s[here, :]
            place = iota((WIN, 1), 0) + row
            inside = (place >= first) & (place < last)
            att_s[here, :] = jnp.where(inside, mix[:, :width] * out + mix[:, width:], att_s[here, :])
            return carry

        return lax.fori_loop(0, windows, window, carry)

    lax.fori_loop(0, GROUPS, group, 0)

    def unplace(i, carry):
        at = pl.ds(pl.multiple_of(i * 128, 128), 128)
        chosen = (iota((128, rows), 1) == rcol[at, :].astype(jnp.int32)).astype(BF16)
        att_out[at, :] = dot(chosen, att_s[:rows, :].astype(BF16)).astype(BF16)
        return carry

    lax.fori_loop(0, tiles, unplace, 0)


def exact_forward(starts, qs, cls, ks, vs, stats, rcol):
    rows, width = rcol.shape[0], qs.shape[1]
    shape = jax.ShapeDtypeStruct
    return pl.pallas_call(
        exact_forward_kernel,
        out_shape=(
            shape((rows, width), BF16),
            shape((CLP, 2 * width), F32),
            shape((CLP, 128), F32),
        ),
        in_specs=[pl.BlockSpec(memory_space=pltpu.SMEM)] + vmem(6),
        out_specs=tuple(vmem(3)),
        scratch_shapes=[
            pltpu.VMEM((rows + WIN, width), F32),
            pltpu.VMEM((rows + WIN, 2 * width), F32),
        ],
        compiler_params=pltpu.CompilerParams(vmem_limit_bytes=40 << 20),
        name="exact_forward",
    )(starts, qs, cls, ks, vs, stats, rcol)


def exact_backward_kernel(
    starts, qs, cls, ks, vs, rows_in, rcol, rrow, grad,
    dq_out, dk_out, dv_out, centre_out,
    grad_s, mass_s, dq_s, part_s, dk_s, dv_s,
):
    rows, width = rcol.shape[0], qs.shape[1]
    heads = width // HEAD_DIM
    tiles = rows // 128
    mass_rows = rows_in[:, :width]
    high = mass_rows.astype(BF16)
    low = (mass_rows - high.astype(F32)).astype(BF16)
    lane = iota((128, 128), 1)
    rank_row = rrow[:1, :].astype(jnp.int32)

    def place(i, carry):
        at = pl.ds(pl.multiple_of(i * 128, 128), 128)
        chosen = (iota((128, rows), 0) + i * 128 == rank_row).astype(BF16)
        grad_s[at, :] = dot(chosen, grad[...]).astype(BF16)
        member = (cls[at, :] == lane).astype(BF16)
        mass_s[at, :] = dot(member, high) + dot(member, low)
        return carry

    lax.fori_loop(0, tiles, place, 0)
    grad_s[rows:, :] = jnp.zeros((WIN, width), BF16)
    mass_s[rows:, :] = jnp.zeros((WIN, width), F32)
    slot_cluster = iota((WIN, GSLOTS), 1) // TOPK

    def group(g, carry):
        at = pl.ds(pl.multiple_of(g * GSLOTS, GSLOTS), GSLOTS)
        keys = block_diagonal(ks[at, :], heads)
        values = block_diagonal(vs[at, :], heads)
        first, last = starts[0, g * GROUP], starts[0, g * GROUP + GROUP]
        base = first // 16 * 16
        windows = jnp.where(last > first, (last - base + WIN - 1) // WIN, 0)
        dk_s[...] = jnp.zeros_like(dk_s)
        dv_s[...] = jnp.zeros_like(dv_s)

        def window(w, carry):
            row = pl.multiple_of(base + w * WIN, 16)
            here = pl.ds(row, WIN)
            mine = cls[here, :] == slot_cluster + g * GROUP
            query, upstream = qs[here, :], grad_s[here, :]
            scores = dot_nt(query, keys) * SCALE
            against = dot_nt(upstream, values)
            mass = mass_s[here, :]
            weights, score_grads = [], []
            mass_part = jnp.zeros((WIN, width), F32)
            for h in range(heads):
                cut = slice(h * GSLOTS, (h + 1) * GSLOTS)
                part = jnp.where(mine, scores[:, cut], NEGATIVE)
                raised = jnp.where(mine, jnp.exp(part - jnp.max(part, 1, keepdims=True)), 0.0)
                total = jnp.maximum(jnp.sum(raised, 1, keepdims=True), 0.5)
                probs = raised / total
                meeting = jnp.sum(probs * against[:, cut], 1, keepdims=True)
                weighted = probs * mass[:, h * HEAD_DIM : h * HEAD_DIM + 1]
                weights.append(weighted.astype(BF16))
                score_grads.append((weighted * (against[:, cut] - meeting)).astype(BF16))
                mass_part = jnp.where(head_lanes(width, h), meeting, mass_part)
            score_grad = jnp.concatenate(score_grads, axis=1)
            weight = jnp.concatenate(weights, axis=1)
            place = iota((WIN, 1), 0) + row
            inside = (place >= first) & (place < last)
            dq = dot(score_grad, keys) * SCALE
            dq_s[here, :] = jnp.where(inside, dq, dq_s[here, :])
            part_s[here, :] = jnp.where(inside, mass_part, part_s[here, :])
            dk_s[...] += diagonal_blocks(dot_tn(score_grad, query), heads) * SCALE
            dv_s[...] += diagonal_blocks(dot_tn(weight, upstream), heads)
            return carry

        lax.fori_loop(0, windows, window, 0)
        dk_out[at, :] = dk_s[...].astype(BF16)
        dv_out[at, :] = dv_s[...].astype(BF16)
        return carry

    lax.fori_loop(0, GROUPS, group, 0)
    centre_out[...] = jnp.zeros_like(centre_out)

    def unplace(i, carry):
        at = pl.ds(pl.multiple_of(i * 128, 128), 128)
        chosen = (iota((128, rows), 1) == rcol[at, :].astype(jnp.int32)).astype(BF16)
        dq_out[at, :] = dot(chosen, dq_s[:rows, :].astype(BF16))
        member = (cls[at, :] == lane).astype(BF16)
        pair = jnp.concatenate([part_s[at, :].astype(BF16), grad_s[at, :]], axis=1)
        centre_out[...] += dot_tn(member, pair)
        return carry

    lax.fori_loop(0, tiles, unplace, 0)


def exact_backward(starts, qs, cls, ks, vs, rows_in, rcol, rrow, grad):
    rows, width = rcol.shape[0], qs.shape[1]
    shape = jax.ShapeDtypeStruct
    return pl.pallas_call(
        exact_backward_kernel,
        out_shape=(
            shape((rows, width), F32),
            shape((SLOTS, width), BF16),
            shape((SLOTS, width), BF16),
            shape((CLP, 2 * width), F32),
        ),
        in_specs=[pl.BlockSpec(memory_space=pltpu.SMEM)] + vmem(8),
        out_specs=tuple(vmem(4)),
        scratch_shapes=[
            pltpu.VMEM((rows + WIN, width), BF16),
            pltpu.VMEM((rows + WIN, width), F32),
            pltpu.VMEM((rows + WIN, width), F32),
            pltpu.VMEM((rows + WIN, width), F32),
            pltpu.VMEM((GSLOTS, width), F32),
            pltpu.VMEM((GSLOTS, width), F32),
        ],
        compiler_params=pltpu.CompilerParams(vmem_limit_bytes=40 << 20),
        name="exact_backward",
    )(starts, qs, cls, ks, vs, rows_in, rcol, rrow, grad)


def centre_backward_kernel(
    lengths, k, v, centre, topk, tm, merged, rows_in, summed, dk_out, dv_out, part_out
):
    rows, width = k.shape
    heads = width // HEAD_DIM
    top = tm[...].astype(F32)
    outside = 1.0 - top
    same = sequence_masks(lengths, topk, rows)
    centre_blocks = block_diagonal(centre[...], heads)
    rest_grad = summed[:, width:].astype(BF16)
    rest_blocks = block_diagonal(rest_grad, heads)
    full = dot_nt(centre_blocks, k[...]) * SCALE
    against = dot_nt(rest_blocks, v[...])
    product = rest_grad.astype(F32) * rows_in[:, width:]
    score_grads, weights = [], []
    for h in range(heads):
        cut = slice(h * CLP, (h + 1) * CLP)
        largest, total = merged[:, h : h + 1], merged[:, 8 + h : 9 + h]
        mass = merged[:, 16 + h : 17 + h]
        mass_grad = summed[:, h * HEAD_DIM : h * HEAD_DIM + 1]
        probs = jnp.where(same, jnp.exp(full[cut] - largest) / total, 0.0)
        mean = mass * mass_grad + jnp.sum(
            jnp.where(head_lanes(width, h), product, 0.0), 1, keepdims=True
        )
        grad = against[cut] * outside + mass_grad * top
        score_grads.append((probs * (grad - mean)).astype(BF16))
        weights.append((probs * outside).astype(BF16))
    score_grad = jnp.concatenate(score_grads, axis=0)
    weight = jnp.concatenate(weights, axis=0)
    part_out[...] = diagonal_blocks(dot(score_grad, k[...]), heads) * SCALE
    dk_out[...] = dot_tn(score_grad, centre_blocks) * SCALE
    dv_out[...] = dot_tn(weight, rest_blocks)


def centre_backward(lengths, k, v, centre, topk, tm, merged, rows_in, summed):
    rows, width = k.shape
    shape = jax.ShapeDtypeStruct
    return pl.pallas_call(
        centre_backward_kernel,
        out_shape=(
            shape((rows, width), F32),
            shape((rows, width), F32),
            shape((CLP, width), F32),
        ),
        in_specs=[pl.BlockSpec(memory_space=pltpu.SMEM)] + vmem(8),
        out_specs=tuple(vmem(3)),
        compiler_params=pltpu.CompilerParams(vmem_limit_bytes=40 << 20),
        name="centre_backward",
    )(lengths, k, v, centre, topk, tm, merged, rows_in, summed)


def gather_kernel(scol, table, out):
    rows = table.shape[0]
    own_start = lax.axis_index("dm") * rows

    def tile(i, carry):
        at = pl.ds(pl.multiple_of(i * 128, 128), 128)
        chosen = (scol[at, :] == iota((128, rows), 1) + own_start).astype(BF16)
        out[at, :] = dot(chosen, table[...]).astype(BF16)
        return carry

    lax.fori_loop(0, SLOTS // 128, tile, 0)


def gather_slots(scol, table):
    return pl.pallas_call(
        gather_kernel,
        out_shape=jax.ShapeDtypeStruct((SLOTS, table.shape[1]), BF16),
        in_specs=vmem(2),
        out_specs=vmem(1)[0],
        compiler_params=pltpu.CompilerParams(vmem_limit_bytes=40 << 20),
        name="gather_slots",
    )(scol, table)


def scatter_kernel(srow, slots, base, out):
    rows = out.shape[0]
    own_start = lax.axis_index("dm") * rows

    def tile(i, carry):
        at = pl.ds(pl.multiple_of(i * 128, 128), 128)
        chosen = (srow[...] == iota((128, SLOTS), 0) + own_start + i * 128).astype(BF16)
        out[at, :] = (base[at, :] + dot(chosen, slots[...])).astype(BF16)
        return carry

    lax.fori_loop(0, rows // 128, tile, 0)


def scatter_slots(srow, slots, base):
    return pl.pallas_call(
        scatter_kernel,
        out_shape=jax.ShapeDtypeStruct(base.shape, BF16),
        in_specs=vmem(3),
        out_specs=vmem(1)[0],
        compiler_params=pltpu.CompilerParams(vmem_limit_bytes=40 << 20),
        name="scatter_slots",
    )(srow, slots, base)


def shards(
    tokens,
    clusters,
    top_keys,
    lengths,
    qkv_weight,
    out_weight,
    first_gain,
    first_bias,
    second_gain,
    second_bias,
    expand_weight,
    shrink_weight,
    cotangent,
):
    row_count = tokens.shape[0]
    width = qkv_weight.shape[2]
    inputs = tokens.astype(F32)
    expand_full, shrink_full = (
        lax.all_gather(expand_weight, ("dp", "dm"), axis=0, tiled=True),
        lax.all_gather(shrink_weight, ("dp", "dm"), axis=1, tiled=True),
    )
    topk = jnp.pad(top_keys, ((0, CLP - CL), (0, 0)), constant_values=-1)
    flat = jnp.pad(top_keys.reshape(-1), (0, SLOTS - CL * TOPK), constant_values=-1)
    scol, srow = flat.reshape(SLOTS, 1), flat.reshape(1, SLOTS)

    first_normed, qs, k, v, csum, starts, rcol, rrow, cls = front(
        tokens, clusters, qkv_weight, first_gain, first_bias
    )
    csum = lax.psum(csum, "dm")
    slot_kv = lax.psum(gather_slots(scol, jnp.concatenate([k, v], axis=1)), "dm")
    ks, vs = slot_kv[:, :width], slot_kv[:, width:]
    centre, tm, stats = centre_forward(lengths, csum, k, v, topk)
    stats = lax.all_gather(stats, "dm", axis=0)
    attended, rows_in, merged = exact_forward(starts, qs, cls, ks, vs, stats, rcol)

    head_part = jnp.dot(attended, out_weight, preferred_element_type=F32)
    attention_sum = lax.psum(head_part.astype(BF16), "hid").astype(F32)
    middle = inputs + attention_sum
    normed_two, spread_two = norm_parts(middle)
    second_normed = (normed_two * second_gain + second_bias).astype(BF16)
    hidden = jnp.dot(second_normed, expand_full, preferred_element_type=F32)
    activated = jax.nn.gelu(hidden).astype(BF16)
    hidden_part = jnp.dot(activated, shrink_full, preferred_element_type=F32)
    hidden_sum = lax.psum(hidden_part.astype(BF16), "hid").astype(F32)
    result = (middle + hidden_sum).astype(BF16)
    upstream = cotangent.astype(F32)
    activated_grad = jnp.dot(cotangent, shrink_full.T, preferred_element_type=F32)
    shrink_local = jnp.dot(activated.T, cotangent, preferred_element_type=F32)
    gelu_value, gelu_pull = jax.vjp(jax.nn.gelu, hidden)
    hidden_grad = gelu_pull(activated_grad)[0].astype(BF16)
    expand_local = jnp.dot(second_normed.T, hidden_grad, preferred_element_type=F32)
    second_part = jnp.dot(hidden_grad, expand_full.T, preferred_element_type=F32)
    second_grad = lax.psum(second_part.astype(BF16), "hid").astype(F32)
    expand_grad, shrink_grad = (
        lax.psum_scatter(expand_local, ("dp", "dm"), scatter_dimension=0, tiled=True),
        lax.psum_scatter(shrink_local, ("dp", "dm"), scatter_dimension=1, tiled=True),
    )
    middle_inner, second_gain_part, second_bias_part = norm_back(
        second_grad, normed_two, spread_two, second_gain
    )
    middle_grad = upstream + middle_inner
    branch_grad = middle_grad.astype(BF16)
    out_grad_part = jnp.dot(attended.T, branch_grad, preferred_element_type=F32)
    attended_grad = jnp.dot(branch_grad, out_weight.T, preferred_element_type=F32).astype(BF16)

    dq, dks, dvs, summed = exact_backward(
        starts, qs, cls, ks, vs, rows_in, rcol, rrow, attended_grad
    )
    summed = lax.psum(summed, "dm")
    dkc, dvc, centre_part = centre_backward(
        lengths, k, v, centre, topk, tm, merged, rows_in, summed
    )
    centre_grad = lax.psum(centre_part, "dm").astype(BF16)
    slot_grads = lax.psum(jnp.concatenate([dks, dvs], axis=1), "dm")
    key_value = scatter_slots(srow, slot_grads, jnp.concatenate([dkc, dvc], axis=1))
    counts = csum[:, width : width + 1]
    member = clusters[:, None] == jnp.arange(CLP, dtype=jnp.int32)[None, :]
    query_centre = jnp.dot(
        member.astype(BF16), centre_grad, preferred_element_type=F32
    ) / jnp.dot(member.astype(F32), counts, precision=HIGHEST)
    query_total = (dq + query_centre).astype(BF16)
    projected_grad = jnp.stack([query_total, key_value[:, :width], key_value[:, width:]])
    projection_part = jnp.einsum(
        "rd,kre->kde", first_normed, projected_grad, preferred_element_type=F32
    )
    first_part = jnp.einsum("kre,kde->rd", projected_grad, qkv_weight, preferred_element_type=F32)
    first_grad = lax.psum(first_part.astype(BF16), "hid").astype(F32)
    normed_one, spread_one = norm_parts(inputs)
    inputs_inner, first_gain_part, first_bias_part = norm_back(
        first_grad, normed_one, spread_one, first_gain
    )
    tokens_grad = (middle_grad + inputs_inner).astype(BF16)
    qkv_grad, out_grad, first_gain_grad, first_bias_grad, second_gain_grad, second_bias_grad = (
        lax.psum(
            (
                projection_part,
                out_grad_part,
                first_gain_part,
                first_bias_part,
                second_gain_part,
                second_bias_part,
            ),
            ("dp", "dm"),
        )
    )
    return (
        result,
        tokens_grad,
        qkv_grad,
        out_grad,
        first_gain_grad,
        first_bias_grad,
        second_gain_grad,
        second_bias_grad,
        expand_grad,
        shrink_grad,
    )


def solution(mesh):
    in_specs = (
        P(("dp", "dm"), None),
        P(("dp", "dm")),
        P("dp", None),
        P("dp"),
        P(None, None, "hid"),
        P("hid", None),
        P(),
        P(),
        P(),
        P(),
        P(("dp", "dm"), "hid"),
        P("hid", ("dp", "dm")),
        P(("dp", "dm"), None),
    )
    out_specs = (
        P(("dp", "dm"), None),
        P(("dp", "dm"), None),
        P(None, None, "hid"),
        P("hid", None),
        P(),
        P(),
        P(),
        P(),
        P(("dp", "dm"), "hid"),
        P("hid", ("dp", "dm")),
    )
    return jax.shard_map(shards, mesh=mesh, in_specs=in_specs, out_specs=out_specs, check_vma=False)
```

time: 2000 us -> 779 us (0.39)
  other arithmetic: 664 us -> 30.7 us
  local copies, waits for them, and re-layouts: 500 us -> 56 us
  matrix products: 222 us -> 52.7 us
  Pallas kernels: 0 us -> 82.9 us
  waiting for transfers between devices: 502 us -> 434 us
    scatter-add x10 -> x0, other arithmetic: 494 us -> none  [the longest x4 227 us: backward_block(): jax.ops.segment_sum(key_rows_part, cluster_block, num_segments=CL)]
    gather x19 -> x0, local copies, waits for them, and re-layouts: 301 us -> none  [the longest x8 139 us: exact_scores(): value_block = cluster_values[cluster_block]]
    dot_general x58 -> x11, matrix products: 213 us -> 45.4 us  [the longest x1 8.07 us: shards(): hidden = jnp.dot(second_normed, expand_full, preferred_element_type=F32)]
    psum x4 -> x7, waiting for transfers between devices: 237 us -> 356 us  [the longest x1 85.5 us: shards(): lax.psum(gather_slots(scol, jnp.concatenate([k, v], axis=1)), 'dm')]
    pallas_call x0 -> x7, Pallas kernels: none -> 82.9 us  [the longest x1 26.3 us: exact_backward(): pl.pallas_call(exact_backward_kernel, out_shape=(shape((rows, width), F32...]
    psum x1, waiting for transfers between devices: 112 us -> 30.9 us  [shards(): lax.psum((projection_part, out_grad_part, first_gain_part, first_bias_par...]
    while x8 -> x0, other arithmetic: 56.5 us -> none
    all_gather x1, waiting for transfers between devices: 39.8 us -> 0.01 us  [shards(): lax.all_gather(expand_weight, ('dp', 'dm'), axis=0, tiled=True)]
  transfers between devices with their start and end apart: 11 -> 12, of which waited for: 9 -> 9; matrix products, arithmetic and copies ran while one was open for 22% -> 8% of each run, Pallas kernels for 0% -> 5%
where the time goes in v1:
time: 779 us; the launch traced here: 769 us
  waiting for transfers between devices  434 us (56%)
  blocking collectives  95.2 us (12%)
  Pallas kernels  82.9 us (11%)
  local copies, waits for them, and re-layouts  56 us (7%)
  matrix products  52.7 us (7%)
  other arithmetic  30.7 us (4%)
  between operations  16.8 us (2%)
    psum x1, waiting for transfers between devices, shards(): lax.psum(gather_slots(scol, jnp.concatenate([k, v], axis=1)), 'dm')  85.5 us
    psum x1, waiting for transfers between devices, shards(): slot_grads = lax.psum(jnp.concatenate([dks, dvs], axis=1), 'dm')  69.7 us
    psum x1, waiting for transfers between devices, shards(): hidden_sum = lax.psum(hidden_part.astype(BF16), 'hid').astype(F32)  59.8 us
    psum x1, waiting for transfers between devices, shards(): second_grad = lax.psum(second_part.astype(BF16), 'hid').astype(F32)  49.2 us
    reduce_scatter x1, waiting for transfers between devices, shards(): lax.psum_scatter(shrink_local, ('dp', 'dm'), scatter_dimension=1, tiled=T...  46.5 us
    unnamed x158, local copies, waits for them, and re-layouts  45.9 us
    psum x1, waiting for transfers between devices, shards(): attention_sum = lax.psum(head_part.astype(BF16), 'hid').astype(F32)  43.8 us
    psum x1, blocking collectives, shards(): lax.psum((projection_part, out_grad_part, first_gain_part, first_bias_par...  39.8 us
  transfers between devices with their start and end apart: 12, of which 9 were waited for; matrix products, arithmetic and copies ran while one was open for 8% of the time, Pallas kernels for 5%

profile of v1, /device:TPU:0, one launch (start us, length us, event | category | flops | bytes accessed | tf_op | source)
XLA Modules:
  0.0 769.5 jit_solution(5123886147420234364)
XLA Ops:
  8.9 1.8 reshape.95.ccol
  12.1 2.3 copy.39.weight
  16.8 13.6 %front.1 = (bf16[1280,768]{1,0:T(8,128)(2,1)S(1)}, bf16[1408,192]{1,0:T(8,128)(2,1)S(1)}, bf16[1280,192]{1,0:T(8,128)(2,1)S(1)}, bf16[1280,192]{1,0:T(8,128)(2,1...) custom-call(bf16[1280,768]{1,0:T(8,128)(2,1)S(1)} %copy-done.2, ...), custom_call_target="tpu_custom_call" | custom-call | tf_op jit(solution)/shard_map/front/pallas_call | solution.py:155
  35.3 2.4 pad_maximum_fusion.3.table
  39.6 10.3 %gather_slots.1 = bf16[3328,384]{1,0:T(8,128)(2,1)S(1)} custom-call(s32[3328,1]{1,0:T(8,128)S(1)} %reshape.96.scol, bf16[1280,384]{1,0:T(8,128)(2,1)S(1)} %copy-done.13), custom_call_target="tpu_custom_call" | custom-call | tf_op jit(solution)/shard_map/gather_slots/pallas_call | solution.py:529
  49.9 1.5 copy-done.7
  52.0 21.1 %all-reduce.16.cloned.1.call-done.csum = f32[128,256]{1,0:T(8,128)} async-done(((f32[128,256]{1,0:T(8,128)}), f32[128,256]{1,0:T(8,128)}) %all-reduce.16.cloned.1.call-update) | async-done | bytes 131088 | tf_op jit(solution)/shard_map/psum | solution.py:592
  75.2 4.8 centre_forward.1
  80.6 30.0 %all-gather = f32[512,384]{1,0:T(8,128)} all-gather(f32[128,384]{1,0:T(8,128)S(1)} %get-tuple-element.38), channel_id=2, replica_groups=mesh['dp'=2,'hid'=4,'dm'=4] {'dm'}, dimensions={0}, use_global_device_ids=true | all-gather | bytes 983040 | tf_op jit(solution)/shard_map/all_gather | solution.py:596
  110.6 85.5 %all-reduce.14.cloned.1.call-done = bf16[3328,384]{1,0:T(8,128)(2,1)} async-done(((bf16[3328,384]{1,0:T(8,128)(2,1)}), bf16[3328,384]{1,0:T(8,128)(2,1)}) %all-reduce.14.cloned.1.call-update) | async-done | bytes 2555920 | tf_op jit(solution)/shard_map/psum | solution.py:593
  196.2 3.0 fusion.49
  199.2 18.7 %exact_forward.1 = (bf16[1280,192]{1,0:T(8,128)(2,1)S(1)}, f32[128,384]{1,0:T(8,128)S(1)}, f32[128,128]{1,0:T(8,128)S(1)}) custom-call(s32[8,128]{1,0:T(8,128)S(1)} %get-tuple-element.32.starts, bf16[1408,192]{1,0:T(8,128)(2,1)S(1)} %copy-done.16, s32[1408,1]{1,0:T(8,128)S(1)} %copy-done.19, bf16[3328,192]{1,0:T(8,128)(2,1)S(1)} %get-tuple-element.72.ks, ...), custom_call_target="tpu_custom_call" | custom-call | tf_op jit(solution)/shard_map/exact_forward/pallas_call | solution.py:331
  220.6 1.9 convolution_convert_fusion
  223.4 5.5 fusion.50
  228.9 43.8 %all-reduce.18.cloned.1.call-done = bf16[1280,768]{1,0:T(8,128)(2,1)} async-done(((bf16[1280,768]{1,0:T(8,128)(2,1)}), bf16[1280,768]{1,0:T(8,128)(2,1)}) %all-reduce.18.cloned.1.call-update) | async-done | bytes 1966096 | tf_op jit(solution)/shard_map/psum | solution.py:600
  272.7 2.3 fusion.28
  276.6 8.1 %fusion.25 = (bf16[1280,768]{1,0:T(8,128)(2,1)S(1)}, f32[1280,768]{1,0:T(8,128)}) fusion(f32[1280,768]{1,0:T(8,128)} %fusion.50, bf16[768,768]{1,0:T(8,128)(2,1)} %all-gather.4.cloned.1.call-done, f32[768]{0:T(1024)} %param.22, f32[768]{0:T(1024)} %param.21, f32[1280]{0:T(1024)} %add_rsqrt_fusion.1, f32[1280]{0:T(1024)} %copy-done.60, ...), kind=kOutput, calls=%fused_computation.36 | convolution fusion | flops 1537474560 | bytes 14958592 | tf_op jit(solution)/shard_map/dot_general | solution.py:604
  286.0 3.0 convolution_convert_fusion.1
  289.2 49.2 %all-reduce.20.cloned.1.call-done = bf16[1280,768]{1,0:T(8,128)(2,1)} async-done(((bf16[1280,768]{1,0:T(8,128)(2,1)}), bf16[1280,768]{1,0:T(8,128)(2,1)}) %all-reduce.20.cloned.1.call-update) | async-done | bytes 1966096 | tf_op jit(solution)/shard_map/psum | solution.py:616
  338.5 5.3 fusion.26
  343.9 3.5 fusion.13
  347.4 2.0 copy-done.47
  349.4 1.6 convolution_convert_fusion.3
  351.0 2.1 copy.43.grad
  360.4 26.3 %exact_backward.1 = (f32[1280,192]{1,0:T(8,128)S(1)}, bf16[3328,192]{1,0:T(8,128)(2,1)S(1)}, bf16[3328,192]{1,0:T(8,128)(2,1)S(1)}, f32[128,384]{1,0:T(8,128)}) custom-call(s32[8,128]{1,0:T(8,128)S(1)} %get-tuple-element.32.starts, bf16[1408,192]{1,0:T(8,128)(2,1)S(1)} %copy-done.17, s32[1408,1]{1,0:T(8,128)S(1)} %copy-done.20, ...), custom_call_target="tpu_custom_call" | custom-call | tf_op jit(solution)/shard_map/exact_backward/pallas_call | solution.py:441
  390.3 4.5 pad_maximum_fusion
  395.6 6.2 convolution_convert_fusion.2
  401.9 26.4 %all-reduce.22.cloned.1.call-done.summed = f32[128,384]{1,0:T(8,128)} async-done(((f32[128,384]{1,0:T(8,128)}), f32[128,384]{1,0:T(8,128)}) %all-reduce.22.cloned.1.call-update) | async-done | bytes 196624 | tf_op jit(solution)/shard_map/psum | solution.py:632
  431.1 3.0 centre_backward.1
  437.0 25.3 %psum.111 = bf16[128,192]{1,0:T(8,128)(2,1)S(1)} all-reduce(f32[128,192]{1,0:T(8,128)} %copy-done.38), channel_id=1, replica_groups=mesh['dp'=2,'hid'=4,'dm'=4] {'dm'}, use_global_device_ids=true, to_apply=%region_12.13 | all-reduce | flops 24576 | bytes 147456 | tf_op jit(solution)/shard_map/psum | solution.py:636
  462.3 2.8 fusion.31
  465.1 1.7 pad_maximum_fusion.1.base
  466.8 69.7 %all-reduce.24.cloned.1.call-done.slots = bf16[3328,384]{1,0:T(8,128)(2,1)} async-done(((bf16[3328,384]{1,0:T(8,128)(2,1)}), bf16[3328,384]{1,0:T(8,128)(2,1)}) %all-reduce.24.cloned.1.call-update) | async-done | bytes 2555920 | tf_op jit(solution)/shard_map/psum | solution.py:637
  536.5 1.5 copy-done.8
  538.1 1.7 copy-done.28
  539.8 6.1 scatter_slots.1
  547.1 3.1 bitcast_convert_fusion
  551.0 5.8 fusion.40
  556.8 6.3 fusion.48
  563.2 3.7 fusion.37
  566.9 4.2 fusion.34
  571.2 59.8 %all-reduce.28.cloned.1.call-done = (bf16[1280,768]{1,0:T(8,128)(2,1)}, bf16[1280,768]{1,0:T(8,128)(2,1)}) async-done(((bf16[1280,768]{1,0:T(8,128)(2,1)}, bf16[1280,768]{1,0:T(8,128)(2,1)}), (bf16[1280,768]{1,0:T(8,128)(2,1)}, bf16[1280,768]{1,0:T(8,128)(2,1)})) %all-reduce.28.cloned.1.call-update) | async-done | bytes 3932176 | tf_op jit(solution)/shard_map/psum | solution.py:607
  631.0 3.3 fusion.27
  634.3 39.8 %all-reduce.2 = (f32[768]{0:T(1024)}, f32[768]{0:T(1024)}, f32[768]{0:T(1024)}, f32[768]{0:T(1024)}) all-reduce(f32[768]{0:T(1024)S(1)} %get-tuple-element.56, f32[768]{0:T(1024)S(1)} %get-tuple-element.62, f32[768]{0:T(1024)S(1)} %copy-done.70, f32[768]{0:T(1024)S(1)} %copy-done.71), channel_id=1, replica_groups=mesh['dp'=2,'hid'=4,'dm'=4] {'dp','dm'}, use_global_device_ids=true, to_apply=%region_20.21 | all-reduce | flops 3072 | bytes 24576 | tf_op jit(solution)/shard_map/psum | solution.py:657
  674.2 6.1 fusion.12
  680.3 46.5 %reduce-scatter.5.cloned.1.call-done = f32[768,96]{0,1:T(8,128)} async-done(((f32[768,768]{0,1:T(8,128)}), f32[768,96]{0,1:T(8,128)}) %reduce-scatter.5.cloned.1.call-update) | async-done | bytes 294928 | tf_op jit(solution)/shard_map/reduce_scatter | solution.py:619
  726.9 30.9 %all-reduce.26.cloned.1.call-done = (f32[3,768,192]{1,2,0:T(8,128)}, f32[192,768]{1,0:T(8,128)}) async-done(((f32[3,768,192]{1,2,0:T(8,128)}, f32[192,768]{1,0:T(8,128)}), (f32[3,768,192]{1,2,0:T(8,128)}, f32[192,768]{1,0:T(8,128)})) %all-reduce.26.cloned.1.call-update) | async-done | bytes 2359312 | tf_op jit(solution)/shard_map/psum | solution.py:657
  757.7 2.9 copy.60
  (198 shorter events, 41.5 us)
Async XLA Ops:
  8.0 212.6 %copy-start = (bf16[192,768]{1,0:T(8,128)(2,1)S(1)}, bf16[192,768]{1,0:T(8,128)(2,1)}, u32[]{:S(2)}) copy-start(bf16[192,768]{1,0:T(8,128)(2,1)} %param.18) | copy-start | bytes 884740
  8.0 6.4 copy-start.2
  8.0 65.1 %all-reduce.16.cloned.1.call-start = ((), (), s32[]{:S(2)}) async-start(), calls=%async_computation.3 | async-start | bytes 262144 | tf_op jit(solution)/shard_map/psum | solution.py:592
  12.1 25.6 %copy-start.72 = (s32[100,32]{0,1:T(8,128)S(1)}, s32[100,32]{0,1:T(8,128)}, u32[]{:S(2)}) copy-start(s32[100,32]{0,1:T(8,128)} %param.15) | copy-start | bytes 38404
  35.2 161.0 %all-reduce.14.cloned.1.call-start = ((), (), s32[]{:S(2)}) async-start(), calls=%async_computation.2 | async-start | bytes 5111808 | tf_op jit(solution)/shard_map/psum | solution.py:593
  37.9 13.5 %copy-start.56 = (s32[3328]{0:T(1024)}, s32[3328]{0:T(1024)S(1)}, u32[]{:S(2)}) copy-start(s32[3328]{0:T(1024)S(1)} %pad.8) | copy-start | bytes 39940
  39.6 33.6 %copy-start.43 = (s32[2]{0:T(128)S(1)}, s32[2]{0:T(128)}, u32[]{:S(2)}) copy-start(s32[2]{0:T(128)} %lengths.3) | copy-start | bytes 28
  51.4 172.0 %all-gather.6.cloned.1.call-start = ((), (), s32[]{:S(2)}) async-start(), calls=%async_computation.6 | async-start | bytes 1327104 | tf_op jit(solution)/shard_map/all_gather | solution.py:583
  52.0 220.7 %all-reduce.18.cloned.1.call-start = ((), (), s32[]{:S(2)}) async-start(), calls=%async_computation.4 | async-start | bytes 3932160 | tf_op jit(solution)/shard_map/psum | solution.py:600
  196.2 3.0 copy-start.14
  196.2 3.0 copy-start.16
  196.2 3.0 copy-start.19
  196.2 3.0 copy-start.26
  199.1 18.8 %copy-start.5 = (bf16[3328,192]{1,0:T(8,128)(2,1)}, bf16[3328,192]{1,0:T(8,128)(2,1)S(1)}, u32[]{:S(2)}) copy-start(bf16[3328,192]{1,0:T(8,128)(2,1)S(1)} %get-tuple-element.72.ks) | copy-start | bytes 3833860
  222.5 54.1 %all-gather.4.cloned.1.call-start = ((), (), s32[]{:S(2)}) async-start(), calls=%async_computation.5 | async-start | bytes 1327104 | tf_op jit(solution)/shard_map/all_gather | solution.py:582
  223.1 115.4 %all-reduce.20.cloned.1.call-start = ((), (), s32[]{:S(2)}) async-start(), calls=%async_computation.7 | async-start | bytes 3932160 | tf_op jit(solution)/shard_map/psum | solution.py:616
  276.6 9.4 %copy-start.73 = (bf16[768,768]{1,0:T(8,128)(2,1)S(1)}, bf16[768,768]{1,0:T(8,128)(2,1)}, u32[]{:S(2)}) copy-start(bf16[768,768]{1,0:T(8,128)(2,1)} %all-gather.4.cloned.1.call-done) | copy-start | bytes 3538948
  289.0 139.3 %all-reduce.22.cloned.1.call-start = ((), (), s32[]{:S(2)}) async-start(), calls=%async_computation.8 | async-start | bytes 393216 | tf_op jit(solution)/shard_map/psum | solution.py:632
  338.5 5.3 copy-start.49
  338.5 5.3 copy-start.50
  338.5 5.4 copy-start.51
  338.5 5.4 copy-start.61
  338.5 5.4 copy-start.63
  338.5 5.4 copy-start.68
  343.8 3.5 copy-start.58
  390.2 146.3 %all-reduce.24.cloned.1.call-start = ((), (), s32[]{:S(2)}) async-start(), calls=%async_computation.9 | async-start | bytes 5111808 | tf_op jit(solution)/shard_map/psum | solution.py:637
  390.3 4.6 copy-start.57
  390.3 4.6 copy-start.36
  390.3 4.8 copy-start.66
  394.8 236.1 %all-reduce.28.cloned.1.call-start = ((), (), s32[]{:S(2)}) async-start(), calls=%async_computation.13 | async-start | bytes 7864320 | tf_op jit(solution)/shard_map/psum | solution.py:607
  395.6 32.7 %copy-start.40 = (bf16[128,192]{1,0:T(8,128)(2,1)S(1)}, bf16[128,192]{1,0:T(8,128)(2,1)}, u32[]{:S(2)}) copy-start(bf16[128,192]{1,0:T(8,128)(2,1)} %copy-done.39) | copy-start | bytes 147460
  462.3 2.8 copy-start.32
  462.3 2.8 copy-start.34
  539.8 7.3 copy-start.52
  539.8 7.3 copy-start.75
  546.2 4.0 copy-start.53
  550.3 130.0 %reduce-scatter.3.cloned.1.call-start = ((), (), s32[]{:S(2)}) async-start(), calls=%async_computation.10 | async-start | bytes 2654208 | tf_op jit(solution)/shard_map/reduce_scatter | solution.py:618
  556.8 6.4 copy-start.22
  556.8 170.1 %reduce-scatter.5.cloned.1.call-start = ((), (), s32[]{:S(2)}) async-start(), calls=%async_computation.11 | async-start | bytes 2654208 | tf_op jit(solution)/shard_map/reduce_scatter | solution.py:619
  563.1 194.6 %all-reduce.26.cloned.1.call-start = ((), (), s32[]{:S(2)}) async-start(), calls=%async_computation.12 | async-start | bytes 4718592 | tf_op jit(solution)/shard_map/psum | solution.py:657
  563.2 3.7 copy-start.45
  566.9 4.3 copy-start.67
  566.9 64.0 %copy-start.59 = (f32[1280]{0:T(1024)S(1)}, f32[1280]{0:T(1024)}, u32[]{:S(2)}) copy-start(f32[1280]{0:T(1024)} %copy-done.58) | copy-start | bytes 15364
  566.9 64.0 %copy-start.65 = (f32[768]{0:T(1024)S(1)}, f32[768]{0:T(1024)}, u32[]{:S(2)}) copy-start(f32[768]{0:T(1024)} %param.19) | copy-start | bytes 9220
  571.2 63.2 %copy-start.70 = (f32[768]{0:T(1024)S(1)}, f32[768]{0:T(1024)}, u32[]{:S(2)}) copy-start(f32[768]{0:T(1024)} %get-tuple-element.54) | copy-start | bytes 9220
  571.2 63.2 %copy-start.71 = (f32[768]{0:T(1024)S(1)}, f32[768]{0:T(1024)}, u32[]{:S(2)}) copy-start(f32[768]{0:T(1024)} %get-tuple-element.60) | copy-start | bytes 9220
  674.2 87.2 %copy-start.1 = (bf16[192,768]{1,0:T(8,128)(2,1)S(1)}, bf16[192,768]{1,0:T(8,128)(2,1)}, u32[]{:S(2)}) copy-start(bf16[192,768]{1,0:T(8,128)(2,1)} %param.18) | copy-start | bytes 884740
  757.7 2.9 copy-start.55
  (41 other events, 45.1 us)
Sparse Core Ops, SparseCore 0:
  35.3 37.7 all-reduce.15
  75.7 120.4 all-reduce.13
  222.6 50.0 all-reduce.17
  289.1 49.3 all-reduce.19
  390.3 37.8 all-reduce.21
  430.7 105.8 all-reduce.23
  550.4 80.4 all-reduce.27
  635.1 122.5 all-reduce.25
Sparse Core Ops, SparseCore 1:
  54.0 92.1 all-gather.5
  225.1 42.1 all-gather.3
  556.9 68.0 reduce-scatter.2
  629.4 97.4 reduce-scatter.4

commit v2 on v1

--- a/solution.py
+++ b/solution.py
@@ -80,17 +80,63 @@
     return out
 
 
+def vmem(n):
+    return [pl.BlockSpec(memory_space=pltpu.VMEM)] * n
+
+
+HALF = SLOTS // 2
+CHUNK = 128
+CHUNKS = HALF // CHUNK
+LAG = 2
+
+
+def small_exchange(buf, sends, recvs, me, parts):
+    copies = []
+    for step in range(1, parts):
+        copies.append(
+            pltpu.make_async_remote_copy(
+                src_ref=buf.at[me],
+                dst_ref=buf.at[me],
+                send_sem=sends.at[step],
+                recv_sem=recvs.at[step],
+                device_id={"dm": lax.rem(me + step, parts)},
+                device_id_type=MESH,
+            )
+        )
+    return copies
+
+
 def front_kernel(
-    tok, ccol, crow, weight, gain, bias,
-    fn_out, qs_out, k_out, v_out, csum_out, starts_out, rcol_out, rrow_out, cls_out,
-    q_ref, member_ref,
+    lengths, tok, ccol, weight, gain, bias, scol, topk,
+    fn_out, sfn_out, qs_out, k_out, v_out, ks_out, vs_out, starts_out, rcol_out, rrow_out,
+    cls_out, centre_out, tm_out, rows_out, merged_out, count_out,
+    q_ref, member_ref, csum, cbuf, rbuf, sbuf, own, to_right, to_left, from_left, from_right,
+    csend, crecv, rsend, rrecv, ssend, srecv,
+    send_right, recv_left, send_left, recv_right, send_x, recv_x, send_core, recv_core,
+    send_relay, recv_relay,
 ):
     rows = tok.shape[0]
     width = weight.shape[2]
+    heads = width // HEAD_DIM
+    half_width = tok.shape[1] // 2
     tiles = rows // 128
+    parts = lax.axis_size("dm")
+    me, hid = lax.axis_index("dm"), lax.axis_index("hid")
+    core, side = lax.rem(hid, 2), hid // 2
+    core_peer = {"hid": hid + 1 - 2 * core}
+    x_peer = {"hid": hid + 2 - 4 * side}
     lower = (iota((128, 128), 0) > iota((128, 128), 1)).astype(BF16)
     lane = iota((128, 128), 1)
-    csum_out[...] = jnp.zeros_like(csum_out)
+
+    barrier = pltpu.get_barrier_semaphore()
+    for step in range(1, parts):
+        pl.semaphore_signal(
+            barrier, inc=1, device_id={"dm": lax.rem(me + step, parts)}, device_id_type=MESH
+        )
+    for peer in (core_peer, x_peer):
+        pl.semaphore_signal(barrier, inc=1, device_id=peer, device_id_type=MESH)
+
+    csum[...] = jnp.zeros_like(csum)
 
     def tile(i, running):
         at = pl.ds(pl.multiple_of(i * 128, 128), 128)
@@ -105,12 +151,122 @@
         low = member.astype(BF16)
         member_ref[at, :] = low
         extended = jnp.concatenate([q, jnp.ones((128, 256 - width), BF16)], axis=1)
-        csum_out[...] += dot_tn(low, extended)
+        csum[...] += dot_tn(low, extended)
         earlier = dot(lower, low) + running
         rcol_out[at, :] = jnp.sum(member * earlier, 1, keepdims=True)
         return running + jnp.sum(member, 0, keepdims=True)
 
     counts = lax.fori_loop(0, tiles, tile, jnp.zeros((1, 128), F32))
+    sums = csum[...]
+    sixteens = jnp.floor(sums * 0.0625)
+    wide = iota((CLP, 256), 1)
+    packed = jnp.where(wide == width, sixteens, jnp.where(wide == width + 1, sums - 16.0 * sixteens, sums))
+    cbuf[me] = packed.astype(BF16)
+    pl.semaphore_wait(barrier, parts + 1)
+    centre_copies = small_exchange(cbuf, csend, crecv, me, parts)
+    for copy in centre_copies:
+        copy.start()
+
+    @pl.when(me == 0)
+    def _():
+        from_left[...] = jnp.zeros_like(from_left)
+
+    @pl.when(me == parts - 1)
+    def _():
+        from_right[...] = jnp.zeros_like(from_right)
+
+    columns = pl.ds(pl.multiple_of(side * half_width, 128), half_width)
+    other_columns = pl.ds(pl.multiple_of((1 - side) * half_width, 128), half_width)
+    own_start = me * rows
+
+    def chunk_rows(i, which):
+        return pl.ds(pl.multiple_of(which * HALF + i * CHUNK, CHUNK), CHUNK)
+
+    def right_copy(i):
+        return pltpu.make_async_remote_copy(
+            src_ref=to_right.at[i], dst_ref=from_left.at[i], send_sem=send_right.at[i],
+            recv_sem=recv_left.at[i], device_id={"dm": lax.rem(me + 1, parts)}, device_id_type=MESH,
+        )
+
+    def left_copy(i):
+        return pltpu.make_async_remote_copy(
+            src_ref=to_left.at[i], dst_ref=from_right.at[i], send_sem=send_left.at[i],
+            recv_sem=recv_right.at[i], device_id={"dm": lax.rem(me + parts - 1, parts)},
+            device_id_type=MESH,
+        )
+
+    def x_copy(i):
+        block = sfn_out.at[chunk_rows(i, core), columns]
+        return pltpu.make_async_remote_copy(
+            src_ref=block, dst_ref=block, send_sem=send_x.at[i], recv_sem=recv_x.at[i],
+            device_id=x_peer, device_id_type=MESH,
+        )
+
+    def core_copy(i):
+        block = sfn_out.at[chunk_rows(i, core), columns]
+        return pltpu.make_async_remote_copy(
+            src_ref=block, dst_ref=block, send_sem=send_core.at[i], recv_sem=recv_core.at[i],
+            device_id=core_peer, device_id_type=MESH,
+        )
+
+    def relay_copy(i):
+        block = sfn_out.at[chunk_rows(i, core), other_columns]
+        return pltpu.make_async_remote_copy(
+            src_ref=block, dst_ref=block, send_sem=send_relay.at[i], recv_sem=recv_relay.at[i],
+            device_id=core_peer, device_id_type=MESH,
+        )
+
+    def when_chunk(i, work):
+        @pl.when((i >= 0) & (i < CHUNKS))
+        def _():
+            work(i)
+
+    def make_own(i):
+        chosen = (scol[chunk_rows(i, core), :] == iota((CHUNK, rows), 1) + own_start).astype(BF16)
+        own[i] = dot(chosen, fn_out[:, columns]).astype(BF16)
+
+    def go_right(i):
+        @pl.when(me > 0)
+        def _():
+            right_copy(i).wait_recv()
+
+        @pl.when(me < parts - 1)
+        def _():
+            to_right[i] = own[i] + from_left[i]
+            right_copy(i).start()
+
+    def go_left(i):
+        @pl.when(me < parts - 1)
+        def _():
+            left_copy(i).wait_recv()
+
+        @pl.when(me > 0)
+        def _():
+            to_left[i] = own[i] + from_right[i]
+            left_copy(i).start()
+
+    def finish(i):
+        sfn_out[chunk_rows(i, core), columns] = own[i] + from_left[i] + from_right[i]
+        x_copy(i).start()
+        core_copy(i).start()
+
+    def relay(i):
+        x_copy(i).wait_recv()
+        relay_copy(i).start()
+
+    far = jnp.maximum(me, parts - 1 - me)
+
+    def ticks(first, last):
+        def tick(t, carry):
+            when_chunk(t, make_own)
+            when_chunk(t - LAG * me, go_right)
+            when_chunk(t - LAG * (parts - 1 - me), go_left)
+            when_chunk(t - LAG * far, finish)
+            when_chunk(t - LAG * far - LAG, relay)
+            return carry
+
+        lax.fori_loop(first, last, tick, 0)
+
     before = (iota((128, 128), 0) < iota((128, 128), 1)).astype(F32)
     starts = jnp.dot(
         jnp.broadcast_to(counts, (8, 128)), before, precision=HIGHEST, preferred_element_type=F32
@@ -126,11 +282,9 @@
         rrow_out[:, at] = turned[:8]
         return carry
 
-    lax.fori_loop(0, tiles, ranks, 0)
-    rank_row = rrow_out[:1, :].astype(jnp.int32)
-
     def place(i, carry):
         at = pl.ds(pl.multiple_of(i * 128, 128), 128)
+        rank_row = rrow_out[:1, :].astype(jnp.int32)
         chosen = (iota((128, rows), 0) + i * 128 == rank_row).astype(BF16)
         qs_out[at, :] = dot(chosen, q_ref[...]).astype(BF16)
         sorted_member = dot(chosen, member_ref[...])
@@ -139,53 +293,24 @@
         )
         return carry
 
-    lax.fori_loop(0, tiles, place, 0)
+    ticks(0, 3)
+    lax.fori_loop(0, tiles, ranks, 0)
+    ticks(3, 5)
+    lax.fori_loop(0, tiles // 2, place, 0)
+    ticks(5, 7)
+    lax.fori_loop(tiles // 2, tiles, place, 0)
     qs_out[rows:, :] = jnp.zeros((WIN, width), BF16)
     cls_out[rows:, :] = jnp.full((WIN, 1), -1, jnp.int32)
-
-
-def vmem(n):
-    return [pl.BlockSpec(memory_space=pltpu.VMEM)] * n
-
-
-def front(tokens, clusters, qkv_weight, gain, bias):
-    rows = tokens.shape[0]
-    width = qkv_weight.shape[2]
-    shape = jax.ShapeDtypeStruct
-    return pl.pallas_call(
-        front_kernel,
-        out_shape=(
-            shape(tokens.shape, BF16),
-            shape((rows + WIN, width), BF16),
-            shape((rows, width), BF16),
-            shape((rows, width), BF16),
-            shape((CLP, 256), F32),
-            shape((8, 128), jnp.int32),
-            shape((rows, 1), F32),
-            shape((8, rows), F32),
-            shape((rows + WIN, 1), jnp.int32),
-        ),
-        in_specs=vmem(6),
-        out_specs=tuple(vmem(9)),
-        scratch_shapes=[pltpu.VMEM((rows, width), BF16), pltpu.VMEM((rows, 128), BF16)],
-        compiler_params=pltpu.CompilerParams(vmem_limit_bytes=40 << 20),
-        name="front",
-    )(tokens, clusters.reshape(rows, 1), clusters.reshape(1, rows), qkv_weight, gain[None], bias[None])
-
-
-def sequence_masks(lengths, topk, rows):
-    own_start = lax.axis_index("dm") * rows
-    key_second = iota((1, rows), 1) + own_start >= lengths[0]
-    centre_second = topk[:, :1] >= lengths[0]
-    return key_second == centre_second
-
-
-def centre_forward_kernel(lengths, csum, k, v, topk, centre_out, tm_out, stat_out):
-    rows, width = k.shape
-    heads = width // HEAD_DIM
-    own_start = lax.axis_index("dm") * rows
-    count = jnp.maximum(csum[:, width : width + 1], 1.0)
-    centre = (csum[:, :width] / count).astype(BF16)
+    ticks(7, 9)
+
+    for copy in centre_copies:
+        copy.wait_recv()
+    gathered = cbuf[0].astype(F32)
+    for d in range(1, parts):
+        gathered += cbuf[d].astype(F32)
+    count = jnp.maximum(16.0 * gathered[:, width : width + 1] + gathered[:, width + 1 : width + 2], 1.0)
+    count_out[...] = jnp.broadcast_to(count, (CLP, 128))
+    centre = (gathered[:, :width] / count).astype(BF16)
     centre_out[...] = centre
     here = iota((CLP, rows), 1) + own_start
     hit = topk[:, :1] == here
@@ -193,10 +318,10 @@
         hit = hit | (topk[:, t : t + 1] == here)
     top = hit.astype(F32)
     tm_out[...] = top.astype(BF16)
+    ticks(9, 11)
     outside = 1.0 - top
     same = sequence_masks(lengths, topk, rows)
-    full = dot_nt(block_diagonal(centre, heads), k[...]) * SCALE
-    lane = iota((CLP, 128), 1)
+    full = dot_nt(block_diagonal(centre, heads), k_out[...]) * SCALE
     stats = jnp.zeros((CLP, 128), F32)
     weights = []
     for h in range(heads):
@@ -209,72 +334,144 @@
         stats = jnp.where(lane == h, largest, stats)
         stats = jnp.where(lane == 8 + h, total, stats)
         stats = jnp.where(lane == 16 + h, mass, stats)
-    rest = diagonal_blocks(dot(jnp.concatenate(weights, axis=0), v[...]), heads)
-    stat_out[:, :256] = jnp.concatenate([rest, jnp.zeros((CLP, 256 - width), F32)], axis=1)
-    stat_out[:, 256:] = stats
-
-
-def centre_forward(lengths, csum, k, v, topk):
-    rows, width = k.shape
+    rest = diagonal_blocks(dot(jnp.concatenate(weights, axis=0), v_out[...]), heads)
+    rbuf[me] = rest.astype(BF16)
+    sbuf[me] = jnp.transpose(stats)[:24]
+    rest_copies = small_exchange(rbuf, rsend, rrecv, me, parts)
+    stat_copies = small_exchange(sbuf, ssend, srecv, me, parts)
+    for copy in rest_copies + stat_copies:
+        copy.start()
+    ticks(11, CHUNKS + LAG * parts)
+
+    for copy in rest_copies + stat_copies:
+        copy.wait_recv()
+    largest = sbuf[0][:8]
+    for d in range(1, parts):
+        largest = jnp.maximum(largest, sbuf[d][:8])
+    total = jnp.zeros((8, 128), F32)
+    mass = jnp.zeros((8, 128), F32)
+    factors = []
+    for d in range(parts):
+        factor = jnp.exp(sbuf[d][:8] - largest)
+        total += factor * sbuf[d][8:16]
+        mass += factor * sbuf[d][16:24]
+        factors.append(factor)
+    live = iota((8, 128), 0) < heads
+    total = jnp.where(live, total, 1.0)
+    mass = mass / total
+    table = [largest, total, mass] + [factor / total for factor in factors]
+    table.append(jnp.zeros((128 - 8 * len(table), 128), F32))
+    columns_table = jnp.transpose(jnp.concatenate(table, axis=0))
+    merged_out[...] = columns_table
+    mass_rows = jnp.zeros((CLP, width), F32)
+    rest_rows = jnp.zeros((CLP, width), F32)
+    for h in range(heads):
+        mine = head_lanes(width, h)
+        mass_rows = jnp.where(mine, columns_table[:, 16 + h : 17 + h], mass_rows)
+        rest = jnp.zeros((CLP, width), F32)
+        for d in range(parts):
+            lane_at = 24 + 8 * d + h
+            rest += columns_table[:, lane_at : lane_at + 1] * rbuf[d].astype(F32)
+        rest_rows = jnp.where(mine, rest, rest_rows)
+    rows_out[:, :width] = mass_rows
+    rows_out[:, width:] = rest_rows
+
+    def arrive(i, carry):
+        core_copy(i).wait_recv()
+        relay_copy(i).wait_recv()
+        return carry
+
+    def project(i, carry):
+        at = pl.ds(pl.multiple_of(i * GSLOTS, GSLOTS), GSLOTS)
+        ks_out[at, :] = dot(sfn_out[at, :], weight[1]).astype(BF16)
+        vs_out[at, :] = dot(sfn_out[at, :], weight[2]).astype(BF16)
+        return carry
+
+    lax.fori_loop(0, CHUNKS, arrive, 0)
+    lax.fori_loop(0, GROUPS, project, 0)
+
+    def drain(i, carry):
+        @pl.when(me < parts - 1)
+        def _():
+            right_copy(i).wait_send()
+
+        @pl.when(me > 0)
+        def _():
+            left_copy(i).wait_send()
+
+        x_copy(i).wait_send()
+        core_copy(i).wait_send()
+        relay_copy(i).wait_send()
+        return carry
+
+    lax.fori_loop(0, CHUNKS, drain, 0)
+    for copy in centre_copies + rest_copies + stat_copies:
+        copy.wait_send()
+
+
+def front(lengths, tokens, clusters, qkv_weight, gain, bias, scol, topk, parts):
+    rows, model = tokens.shape
+    width = qkv_weight.shape[2]
     shape = jax.ShapeDtypeStruct
+    dma = pltpu.SemaphoreType.DMA
+    chain = pltpu.VMEM((CHUNKS, CHUNK, model // 2), BF16)
     return pl.pallas_call(
-        centre_forward_kernel,
+        front_kernel,
         out_shape=(
+            shape(tokens.shape, BF16),
+            shape((SLOTS, model), BF16),
+            shape((rows + WIN, width), BF16),
+            shape((rows, width), BF16),
+            shape((rows, width), BF16),
+            shape((SLOTS, width), BF16),
+            shape((SLOTS, width), BF16),
+            shape((8, 128), jnp.int32),
+            shape((rows, 1), F32),
+            shape((8, rows), F32),
+            shape((rows + WIN, 1), jnp.int32),
             shape((CLP, width), BF16),
             shape((CLP, rows), BF16),
-            shape((CLP, 384), F32),
+            shape((CLP, 2 * width), F32),
+            shape((CLP, 128), F32),
+            shape((CLP, 128), F32),
         ),
-        in_specs=[pl.BlockSpec(memory_space=pltpu.SMEM)] + vmem(4),
-        out_specs=tuple(vmem(3)),
-        compiler_params=pltpu.CompilerParams(vmem_limit_bytes=40 << 20),
-        name="centre_forward",
-    )(lengths, csum, k, v, topk)
-
-
-def merge_stats(stats, heads, width):
-    parts = stats.shape[0]
-    largest = stats[0][:, 256:]
-    for d in range(1, parts):
-        largest = jnp.maximum(largest, stats[d][:, 256:])
-    total = jnp.zeros((CLP, 1), F32)
-    mass_rows = jnp.zeros((CLP, width), F32)
-    rest_rows = jnp.zeros((CLP, width), F32)
-    lane = iota((CLP, 128), 1)
-    merged = jnp.zeros((CLP, 128), F32)
-    for h in range(heads):
-        top = largest[:, h : h + 1]
-        total = jnp.zeros((CLP, 1), F32)
-        mass = jnp.zeros((CLP, 1), F32)
-        rest = jnp.zeros((CLP, width), F32)
-        for d in range(parts):
-            block = stats[d]
-            factor = jnp.exp(block[:, 256 + h : 257 + h] - top)
-            total += factor * block[:, 264 + h : 265 + h]
-            mass += factor * block[:, 272 + h : 273 + h]
-            rest += factor * block[:, :width]
-        mine = head_lanes(width, h)
-        mass = mass / total
-        mass_rows = jnp.where(mine, mass, mass_rows)
-        rest_rows = jnp.where(mine, rest / total, rest_rows)
-        merged = jnp.where(lane == h, top, merged)
-        merged = jnp.where(lane == 8 + h, total, merged)
-        merged = jnp.where(lane == 16 + h, mass, merged)
-    return mass_rows, rest_rows, merged
+        in_specs=[pl.BlockSpec(memory_space=pltpu.SMEM)] + vmem(7),
+        out_specs=tuple(vmem(16)),
+        scratch_shapes=[
+            pltpu.VMEM((rows, width), BF16),
+            pltpu.VMEM((rows, 128), BF16),
+            pltpu.VMEM((CLP, 256), F32),
+            pltpu.VMEM((parts, CLP, 256), BF16),
+            pltpu.VMEM((parts, CLP, width), BF16),
+            pltpu.VMEM((parts, 24, 128), F32),
+            chain, chain, chain, chain, chain,
+        ]
+        + [dma((parts,))] * 6
+        + [dma((CHUNKS,))] * 10,
+        compiler_params=pltpu.CompilerParams(
+            vmem_limit_bytes=56 << 20, collective_id=0, has_side_effects=True
+        ),
+        name="front",
+    )(
+        lengths, tokens, clusters.reshape(rows, 1), qkv_weight, gain[None], bias[None], scol, topk
+    )
+
+
+def sequence_masks(lengths, topk, rows):
+    own_start = lax.axis_index("dm") * rows
+    key_second = iota((1, rows), 1) + own_start >= lengths[0]
+    centre_second = topk[:, :1] >= lengths[0]
+    return key_second == centre_second
 
 
 def exact_forward_kernel(
-    starts, qs, cls, ks, vs, stats, rcol, att_out, rows_out, merged_out, att_s, mix_s
+    starts, qs, cls, ks, vs, both, rcol, att_out, att_s, mix_s
 ):
     rows, width = rcol.shape[0], qs.shape[1]
     heads = width // HEAD_DIM
     tiles = rows // 128
-    mass_rows, rest_rows, merged = merge_stats(stats, heads, width)
-    rows_out[:, :width] = mass_rows
-    rows_out[:, width:] = rest_rows
-    merged_out[...] = merged
-    both = jnp.concatenate([mass_rows, rest_rows], axis=1)
-    high = both.astype(BF16)
-    low = (both - high.astype(F32)).astype(BF16)
+    high = both[...].astype(BF16)
+    low = (both[...] - high.astype(F32)).astype(BF16)
     lane = iota((128, 128), 1)
 
     def spread(i, carry):
@@ -325,25 +522,21 @@
     lax.fori_loop(0, tiles, unplace, 0)
 
 
-def exact_forward(starts, qs, cls, ks, vs, stats, rcol):
+def exact_forward(starts, qs, cls, ks, vs, both, rcol):
     rows, width = rcol.shape[0], qs.shape[1]
     shape = jax.ShapeDtypeStruct
     return pl.pallas_call(
         exact_forward_kernel,
-        out_shape=(
-            shape((rows, width), BF16),
-            shape((CLP, 2 * width), F32),
-            shape((CLP, 128), F32),
-        ),
+        out_shape=shape((rows, width), BF16),
         in_specs=[pl.BlockSpec(memory_space=pltpu.SMEM)] + vmem(6),
-        out_specs=tuple(vmem(3)),
+        out_specs=vmem(1)[0],
         scratch_shapes=[
             pltpu.VMEM((rows + WIN, width), F32),
             pltpu.VMEM((rows + WIN, 2 * width), F32),
         ],
         compiler_params=pltpu.CompilerParams(vmem_limit_bytes=40 << 20),
         name="exact_forward",
-    )(starts, qs, cls, ks, vs, stats, rcol)
+    )(starts, qs, cls, ks, vs, both, rcol)
 
 
 def exact_backward_kernel(
@@ -512,30 +705,6 @@
     )(lengths, k, v, centre, topk, tm, merged, rows_in, summed)
 
 
-def gather_kernel(scol, table, out):
-    rows = table.shape[0]
-    own_start = lax.axis_index("dm") * rows
-
-    def tile(i, carry):
-        at = pl.ds(pl.multiple_of(i * 128, 128), 128)
-        chosen = (scol[at, :] == iota((128, rows), 1) + own_start).astype(BF16)
-        out[at, :] = dot(chosen, table[...]).astype(BF16)
-        return carry
-
-    lax.fori_loop(0, SLOTS // 128, tile, 0)
-
-
-def gather_slots(scol, table):
-    return pl.pallas_call(
-        gather_kernel,
-        out_shape=jax.ShapeDtypeStruct((SLOTS, table.shape[1]), BF16),
-        in_specs=vmem(2),
-        out_specs=vmem(1)[0],
-        compiler_params=pltpu.CompilerParams(vmem_limit_bytes=40 << 20),
-        name="gather_slots",
-    )(scol, table)
-
-
 def scatter_kernel(srow, slots, base, out):
     rows = out.shape[0]
     own_start = lax.axis_index("dm") * rows
@@ -586,15 +755,13 @@
     flat = jnp.pad(top_keys.reshape(-1), (0, SLOTS - CL * TOPK), constant_values=-1)
     scol, srow = flat.reshape(SLOTS, 1), flat.reshape(1, SLOTS)
 
-    first_normed, qs, k, v, csum, starts, rcol, rrow, cls = front(
-        tokens, clusters, qkv_weight, first_gain, first_bias
-    )
-    csum = lax.psum(csum, "dm")
-    slot_kv = lax.psum(gather_slots(scol, jnp.concatenate([k, v], axis=1)), "dm")
-    ks, vs = slot_kv[:, :width], slot_kv[:, width:]
-    centre, tm, stats = centre_forward(lengths, csum, k, v, topk)
-    stats = lax.all_gather(stats, "dm", axis=0)
-    attended, rows_in, merged = exact_forward(starts, qs, cls, ks, vs, stats, rcol)
+    (
+        first_normed, slot_normed, qs, k, v, ks, vs, starts, rcol, rrow, cls, centre, tm, rows_in,
+        merged, counts,
+    ) = front(
+        lengths, tokens, clusters, qkv_weight, first_gain, first_bias, scol, topk, lax.axis_size("dm")
+    )
+    attended = exact_forward(starts, qs, cls, ks, vs, rows_in, rcol)
 
     head_part = jnp.dot(attended, out_weight, preferred_element_type=F32)
     attention_sum = lax.psum(head_part.astype(BF16), "hid").astype(F32)
@@ -636,11 +803,10 @@
     centre_grad = lax.psum(centre_part, "dm").astype(BF16)
     slot_grads = lax.psum(jnp.concatenate([dks, dvs], axis=1), "dm")
     key_value = scatter_slots(srow, slot_grads, jnp.concatenate([dkc, dvc], axis=1))
-    counts = csum[:, width : width + 1]
     member = clusters[:, None] == jnp.arange(CLP, dtype=jnp.int32)[None, :]
     query_centre = jnp.dot(
         member.astype(BF16), centre_grad, preferred_element_type=F32
-    ) / jnp.dot(member.astype(F32), counts, precision=HIGHEST)
+    ) / jnp.dot(member.astype(F32), counts[:, :1], precision=HIGHEST)
     query_total = (dq + query_centre).astype(BF16)
     projected_grad = jnp.stack([query_total, key_value[:, :width], key_value[:, width:]])
     projection_part = jnp.einsum(

time: 779 us -> 707 us (0.908)
  waiting for transfers between devices: 434 us -> 360 us
  Pallas kernels: 82.9 us -> 133 us
  blocking collectives: 95.2 us -> 64.6 us
  local copies, waits for them, and re-layouts: 56 us -> 44.3 us
    psum x2 -> x0, waiting for transfers between devices: 107 us -> none  [the longest x1 85.5 us: shards(): lax.psum(gather_slots(scol, jnp.concatenate([k, v], axis=1)), 'dm')]
    pallas_call x1, Pallas kernels: 13.6 us -> 79.1 us  [front(): pl.pallas_call(front_kernel, out_shape=(shape(tokens.shape, BF16), shape(...]
    all_gather x1 -> x0, blocking collectives: 30 us -> none  [shards(): stats = lax.all_gather(stats, 'dm', axis=0)]
    all_gather x1, waiting for transfers between devices: 0.01 us -> 27.7 us  [shards(): lax.all_gather(expand_weight, ('dp', 'dm'), axis=0, tiled=True)]
    pallas_call x3 -> x1, Pallas kernels: 33.8 us -> 18.1 us  [exact_forward(): pl.pallas_call(exact_forward_kernel, out_shape=shape((rows, width), BF16)...]
    unnamed x158 -> x114, local copies, waits for them, and re-layouts: 45.9 us -> 34.4 us
  transfers between devices with their start and end apart: 12 -> 10, of which waited for: 9 -> 8; matrix products, arithmetic and copies ran while one was open for 8% -> 8% of each run, Pallas kernels for 5% -> 0%
where the time goes in v2:
time: 707 us; the launch traced here: 697 us
  waiting for transfers between devices  360 us (51%)
  Pallas kernels  133 us (19%)
  blocking collectives  64.6 us (9%)
  matrix products  52.6 us (7%)
  local copies, waits for them, and re-layouts  44.3 us (6%)
  other arithmetic  25.4 us (4%)
  between operations  16.5 us (2%)
    pallas_call x1, Pallas kernels, front(): pl.pallas_call(front_kernel, out_shape=(shape(tokens.shape, BF16), shape(...  79.1 us
    psum x1, waiting for transfers between devices, shards(): slot_grads = lax.psum(jnp.concatenate([dks, dvs], axis=1), 'dm')  73.9 us
    psum x1, waiting for transfers between devices, shards(): hidden_sum = lax.psum(hidden_part.astype(BF16), 'hid').astype(F32)  59 us
    psum x1, waiting for transfers between devices, shards(): attention_sum = lax.psum(head_part.astype(BF16), 'hid').astype(F32)  49 us
    psum x1, waiting for transfers between devices, shards(): second_grad = lax.psum(second_part.astype(BF16), 'hid').astype(F32)  47.4 us
    reduce_scatter x1, waiting for transfers between devices, shards(): lax.psum_scatter(shrink_local, ('dp', 'dm'), scatter_dimension=1, tiled=T...  46.6 us
    psum x1, blocking collectives, shards(): lax.psum((projection_part, out_grad_part, first_gain_part, first_bias_par...  40.2 us
    unnamed x114, local copies, waits for them, and re-layouts  34.4 us
  transfers between devices with their start and end apart: 10, of which 8 were waited for; matrix products, arithmetic and copies ran while one was open for 8% of the time, Pallas kernels for 0%

profile of v2, /device:TPU:0, one launch (start us, length us, event | category | flops | bytes accessed | tf_op | source)
XLA Modules:
  0.0 697.0 jit_solution(14417916174658757235)
XLA Ops:
  8.1 1.3 broadcast_in_dim.5.bias
  9.4 1.3 broadcast_in_dim.4.gain
  12.2 1.8 reshape.90.ccol
  14.0 2.3 copy.41.weight
  16.3 2.3 reshape.91.scol
  18.6 79.1 %front.1 = (bf16[1280,768]{1,0:T(8,128)(2,1)}, bf16[3328,768]{1,0:T(8,128)(2,1)}, bf16[1408,192]{1,0:T(8,128)(2,1)}, bf16[1280,192]{1,0:T(8,128)(2,1)}, bf16[128...) custom-call(s32[2]{0:T(128)} %lengths.3, ...), custom_call_target="tpu_custom_call" | custom-call | tf_op jit(solution)/shard_map/front/pallas_call | solution.py:418
  97.7 1.4 copy-done.2
  99.2 1.5 copy-done.4
  105.5 18.1 %exact_forward.1 = bf16[1280,192]{1,0:T(8,128)(2,1)S(1)} custom-call(s32[8,128]{1,0:T(8,128)S(1)} %copy-done.31, bf16[1408,192]{1,0:T(8,128)(2,1)S(1)} %copy-done.6, s32[1408,1]{1,0:T(8,128)S(1)} %copy-done.8, bf16[3328,192]{1,0:T(8,128)(2,1)S(1)} %copy-done.2, bf16[3328,192]{1,0:T(8,128)(2,1)S(1)} %copy-done.4, f32[128,384]{1,0:T(8,128)S(1)} %copy-done.14, ...), custom_call_target="tpu_custom_call" | custom-call | tf_op jit(solution)/shard_map/exact_forward/pallas_call | solution.py:528
  123.6 1.9 convolution_convert_fusion
  127.0 49.0 %all-reduce.12.cloned.1.call-done = bf16[1280,768]{1,0:T(8,128)(2,1)} async-done(((bf16[1280,768]{1,0:T(8,128)(2,1)}), bf16[1280,768]{1,0:T(8,128)(2,1)}) %all-reduce.12.cloned.1.call-update) | async-done | bytes 1966096 | tf_op jit(solution)/shard_map/psum | solution.py:767
  176.0 2.3 fusion.28
  179.3 5.5 fusion.49
  184.8 27.7 %all-gather.3.cloned.1.call-done = bf16[768,768]{1,0:T(8,128)(2,1)} async-done(((bf16[96,768]{1,0:T(8,128)(2,1)}), bf16[768,768]{1,0:T(8,128)(2,1)}) %all-gather.3.cloned.1.call-update) | async-done | bytes 1179664 | tf_op jit(solution)/shard_map/all_gather | solution.py:751
  212.5 8.0 %fusion.25 = (bf16[1280,768]{1,0:T(8,128)(2,1)S(1)}, f32[1280,768]{1,0:T(8,128)}) fusion(f32[1280,768]{1,0:T(8,128)} %fusion.49, bf16[768,768]{1,0:T(8,128)(2,1)} %all-gather.3.cloned.1.call-done, f32[768]{0:T(1024)S(1)} %copy-done.52, f32[768]{0:T(1024)S(1)} %copy-done.48, f32[1280]{0:T(1024)S(1)} %add_rsqrt_fusion.1, ...), kind=kOutput, calls=%fused_computation.36 | convolution fusion | flops 1537474560 | bytes 14958592 | tf_op jit(solution)/shard_map/dot_general | solution.py:771
  220.5 1.3 copy-done.54
  221.8 3.0 convolution_convert_fusion.1
  225.2 47.4 %all-reduce.14.cloned.1.call-done = bf16[1280,768]{1,0:T(8,128)(2,1)} async-done(((bf16[1280,768]{1,0:T(8,128)(2,1)}), bf16[1280,768]{1,0:T(8,128)(2,1)}) %all-reduce.14.cloned.1.call-update) | async-done | bytes 1966096 | tf_op jit(solution)/shard_map/psum | solution.py:783
  272.7 4.7 fusion.26
  277.5 2.9 fusion.13
  280.4 2.0 copy-done.37
  282.4 1.6 convolution_convert_fusion.3
  284.0 2.1 copy.43.grad
  286.1 1.4 copy-done.5
  291.8 26.3 %exact_backward.1 = (f32[1280,192]{1,0:T(8,128)S(1)}, bf16[3328,192]{1,0:T(8,128)(2,1)S(1)}, bf16[3328,192]{1,0:T(8,128)(2,1)S(1)}, f32[128,384]{1,0:T(8,128)}) custom-call(s32[8,128]{1,0:T(8,128)S(1)} %copy-done.32, bf16[1408,192]{1,0:T(8,128)(2,1)S(1)} %copy-done.7, s32[1408,1]{1,0:T(8,128)S(1)} %copy-done.9, bf16[3328,192]{1,0:T(8,128)(2,1)S(1)} %copy-done.3, ...), custom_call_target="tpu_custom_call" | custom-call | tf_op jit(solution)/shard_map/exact_backward/pallas_call | solution.py:634
  318.1 1.2 copy-done.17
  321.7 4.5 pad_maximum_fusion
  327.0 6.3 convolution_convert_fusion.2
  333.4 27.2 %all-reduce.16.cloned.1.call-done.summed = f32[128,384]{1,0:T(8,128)} async-done(((f32[128,384]{1,0:T(8,128)}), f32[128,384]{1,0:T(8,128)}) %all-reduce.16.cloned.1.call-update) | async-done | bytes 196624 | tf_op jit(solution)/shard_map/psum | solution.py:799
  361.5 3.0 centre_backward.1
  366.7 24.5 %psum.95 = bf16[128,192]{1,0:T(8,128)(2,1)S(1)} all-reduce(f32[128,192]{1,0:T(8,128)S(1)} %get-tuple-element.47), channel_id=1, replica_groups=mesh['dp'=2,'hid'=4,'dm'=4] {'dm'}, use_global_device_ids=true, to_apply=%region_10.11 | all-reduce | flops 24576 | bytes 147456 | tf_op jit(solution)/shard_map/psum | solution.py:803
  391.2 2.7 fusion.31
  394.3 73.9 %all-reduce.18.cloned.1.call-done.slots = bf16[3328,384]{1,0:T(8,128)(2,1)} async-done(((bf16[3328,384]{1,0:T(8,128)(2,1)}), bf16[3328,384]{1,0:T(8,128)(2,1)}) %all-reduce.18.cloned.1.call-update) | async-done | bytes 2555920 | tf_op jit(solution)/shard_map/psum | solution.py:804
  468.2 1.7 copy-done.13
  469.9 6.1 scatter_slots.1
  477.4 3.1 bitcast_convert_fusion
  480.6 1.5 copy-done.36
  482.1 5.8 fusion.40
  487.9 6.3 fusion.48
  494.3 3.7 fusion.37
  497.9 4.2 fusion.34
  502.2 59.0 %all-reduce.22.cloned.1.call-done = (bf16[1280,768]{1,0:T(8,128)(2,1)}, bf16[1280,768]{1,0:T(8,128)(2,1)}) async-done(((bf16[1280,768]{1,0:T(8,128)(2,1)}, bf16[1280,768]{1,0:T(8,128)(2,1)}), (bf16[1280,768]{1,0:T(8,128)(2,1)}, bf16[1280,768]{1,0:T(8,128)(2,1)})) %all-reduce.22.cloned.1.call-update) | async-done | bytes 3932176 | tf_op jit(solution)/shard_map/psum | solution.py:774
  561.2 3.3 fusion.27
  564.6 40.2 %all-reduce.2 = (f32[768]{0:T(1024)}, f32[768]{0:T(1024)}, f32[768]{0:T(1024)}, f32[768]{0:T(1024)}) all-reduce(f32[768]{0:T(1024)S(1)} %get-tuple-element.56, f32[768]{0:T(1024)S(1)} %get-tuple-element.62, f32[768]{0:T(1024)S(1)} %get-tuple-element.54, ...), channel_id=1, replica_groups=mesh['dp'=2,'hid'=4,'dm'=4] {'dp','dm'}, use_global_device_ids=true, to_apply=%region_18.19 | all-reduce | flops 3072 | bytes 24576 | tf_op jit(solution)/shard_map/psum | solution.py:823
  604.7 6.2 fusion.12
  610.9 46.6 %reduce-scatter.5.cloned.1.call-done = f32[768,96]{0,1:T(8,128)} async-done(((f32[768,768]{0,1:T(8,128)}), f32[768,96]{0,1:T(8,128)}) %reduce-scatter.5.cloned.1.call-update) | async-done | bytes 294928 | tf_op jit(solution)/shard_map/reduce_scatter | solution.py:786
  657.6 27.9 %all-reduce.20.cloned.1.call-done = (f32[3,768,192]{1,2,0:T(8,128)}, f32[192,768]{1,0:T(8,128)}) async-done(((f32[3,768,192]{1,2,0:T(8,128)}, f32[192,768]{1,0:T(8,128)}), (f32[3,768,192]{1,2,0:T(8,128)}, f32[192,768]{1,0:T(8,128)})) %all-reduce.20.cloned.1.call-update) | async-done | bytes 2359312 | tf_op jit(solution)/shard_map/psum | solution.py:823
  685.5 2.9 copy.58
  (142 shorter events, 22.6 us)
Async XLA Ops:
  8.0 115.6 %copy-start = (bf16[192,768]{1,0:T(8,128)(2,1)S(1)}, bf16[192,768]{1,0:T(8,128)(2,1)}, u32[]{:S(2)}) copy-start(bf16[192,768]{1,0:T(8,128)(2,1)} %param.18) | copy-start | bytes 884740
  8.0 167.9 %all-reduce.12.cloned.1.call-start = ((), (), s32[]{:S(2)}) async-start(), calls=%async_computation.2 | async-start | bytes 3932160 | tf_op jit(solution)/shard_map/psum | solution.py:767
  97.7 1.5 copy-start.2
  99.2 1.5 copy-start.4
  123.6 52.4 %copy-start.35 = (bf16[1280,768]{1,0:T(8,128)(2,1)S(1)}, bf16[1280,768]{1,0:T(8,128)(2,1)}, u32[]{:S(2)}) copy-start(bf16[1280,768]{1,0:T(8,128)(2,1)} %tok.1) | copy-start | bytes 5898244
  125.6 53.7 %all-gather.5.cloned.1.call-start = ((), (), s32[]{:S(2)}) async-start(), calls=%async_computation.4 | async-start | bytes 1327104 | tf_op jit(solution)/shard_map/all_gather | solution.py:752
  126.1 86.3 %all-gather.3.cloned.1.call-start = ((), (), s32[]{:S(2)}) async-start(), calls=%async_computation.3 | async-start | bytes 1327104 | tf_op jit(solution)/shard_map/all_gather | solution.py:751
  126.7 145.9 %all-reduce.14.cloned.1.call-start = ((), (), s32[]{:S(2)}) async-start(), calls=%async_computation.5 | async-start | bytes 3932160 | tf_op jit(solution)/shard_map/psum | solution.py:783
  176.0 2.3 copy-start.38
  179.2 33.2 %copy-start.48 = (f32[768]{0:T(1024)S(1)}, f32[768]{0:T(1024)}, u32[]{:S(2)}) copy-start(f32[768]{0:T(1024)} %param.21) | copy-start | bytes 9220
  179.3 33.2 %copy-start.52 = (f32[768]{0:T(1024)S(1)}, f32[768]{0:T(1024)}, u32[]{:S(2)}) copy-start(f32[768]{0:T(1024)} %param.22) | copy-start | bytes 9220
  212.5 9.3 %copy-start.51 = (bf16[768,768]{1,0:T(8,128)(2,1)S(1)}, bf16[768,768]{1,0:T(8,128)(2,1)}, u32[]{:S(2)}) copy-start(bf16[768,768]{1,0:T(8,128)(2,1)} %all-gather.3.cloned.1.call-done) | copy-start | bytes 3538948
  220.5 1.3 copy-start.54
  224.8 135.8 %all-reduce.16.cloned.1.call-start = ((), (), s32[]{:S(2)}) async-start(), calls=%async_computation.6 | async-start | bytes 393216 | tf_op jit(solution)/shard_map/psum | solution.py:799
  272.7 4.8 copy-start.39
  272.7 4.8 copy-start.40
  272.7 4.8 copy-start.41
  280.4 2.0 copy-start.37
  280.4 5.7 copy-start.3
  280.4 5.7 copy-start.7
  280.4 5.7 copy-start.30
  280.4 5.7 copy-start.32
  286.1 1.5 copy-start.5
  321.6 146.6 %all-reduce.18.cloned.1.call-start = ((), (), s32[]{:S(2)}) async-start(), calls=%async_computation.7 | async-start | bytes 5111808 | tf_op jit(solution)/shard_map/psum | solution.py:804
  321.6 4.7 copy-start.46
  321.6 4.8 copy-start.49
  326.2 235.0 %all-reduce.22.cloned.1.call-start = ((), (), s32[]{:S(2)}) async-start(), calls=%async_computation.11 | async-start | bytes 7864320 | tf_op jit(solution)/shard_map/psum | solution.py:774
  327.0 33.6 %copy-start.16 = (f32[128,384]{1,0:T(8,128)S(1)}, f32[128,384]{1,0:T(8,128)}, u32[]{:S(2)}) copy-start(f32[128,384]{1,0:T(8,128)} %get-tuple-element.37.both.rows_in) | copy-start | bytes 589828
  327.0 33.6 %copy-start.23 = (bf16[1280,192]{1,0:T(8,128)(2,1)S(1)}, bf16[1280,192]{1,0:T(8,128)(2,1)}, u32[]{:S(2)}) copy-start(bf16[1280,192]{1,0:T(8,128)(2,1)} %get-tuple-element.41.k) | copy-start | bytes 1474564
  327.0 33.6 %copy-start.24 = (bf16[1280,192]{1,0:T(8,128)(2,1)S(1)}, bf16[1280,192]{1,0:T(8,128)(2,1)}, u32[]{:S(2)}) copy-start(bf16[1280,192]{1,0:T(8,128)(2,1)} %get-tuple-element.42.v) | copy-start | bytes 1474564
  327.0 33.6 %copy-start.25 = (s32[128,32]{1,0:T(8,128)S(1)}, s32[128,32]{1,0:T(8,128)}, u32[]{:S(2)}) copy-start(s32[128,32]{1,0:T(8,128)} %pad.9.topk) | copy-start | bytes 49156
  327.0 33.6 %copy-start.26 = (bf16[128,1280]{1,0:T(8,128)(2,1)S(1)}, bf16[128,1280]{1,0:T(8,128)(2,1)}, u32[]{:S(2)}) copy-start(bf16[128,1280]{1,0:T(8,128)(2,1)} %get-tuple-element.44.tm) | copy-start | bytes 983044
  327.0 33.6 %copy-start.28 = (bf16[128,192]{1,0:T(8,128)(2,1)S(1)}, bf16[128,192]{1,0:T(8,128)(2,1)}, u32[]{:S(2)}) copy-start(bf16[128,192]{1,0:T(8,128)(2,1)} %get-tuple-element.43.centre) | copy-start | bytes 147460
  327.0 33.6 %copy-start.29 = (f32[128,128]{1,0:T(8,128)S(1)}, f32[128,128]{1,0:T(8,128)}, u32[]{:S(2)}) copy-start(f32[128,128]{1,0:T(8,128)} %get-tuple-element.45.merged) | copy-start | bytes 196612
  327.0 33.6 %copy-start.33 = (s32[2]{0:T(128)S(1)}, s32[2]{0:T(128)}, u32[]{:S(2)}) copy-start(s32[2]{0:T(128)} %lengths.3) | copy-start | bytes 28
  391.2 2.8 copy-start.20
  391.2 2.8 copy-start.22
  468.2 1.7 copy-start.13
  469.9 7.5 %copy-start.42 = (bf16[3,768,192]{1,2,0:T(8,128)(2,1)S(1)}, bf16[3,768,192]{1,2,0:T(8,128)(2,1)}, u32[]{:S(2)}) copy-start(bf16[3,768,192]{1,2,0:T(8,128)(2,1)} %param.17) | copy-start | bytes 2654212
  469.9 7.5 %copy-start.53 = (bf16[1,1280,192]{2,1,0:T(8,128)(2,1)S(1)}, bf16[1,1280,192]{2,1,0:T(8,128)(2,1)}, u32[]{:S(2)}) copy-start(bf16[1,1280,192]{2,1,0:T(8,128)(2,1)} %fusion.31) | copy-start | bytes 1474564
  480.5 1.5 copy-start.36
  480.6 130.4 %reduce-scatter.3.cloned.1.call-start = ((), (), s32[]{:S(2)}) async-start(), calls=%async_computation.8 | async-start | bytes 2654208 | tf_op jit(solution)/shard_map/reduce_scatter | solution.py:785
  487.9 169.7 %reduce-scatter.5.cloned.1.call-start = ((), (), s32[]{:S(2)}) async-start(), calls=%async_computation.9 | async-start | bytes 2654208 | tf_op jit(solution)/shard_map/reduce_scatter | solution.py:786
  494.2 191.3 %all-reduce.20.cloned.1.call-start = ((), (), s32[]{:S(2)}) async-start(), calls=%async_computation.10 | async-start | bytes 4718592 | tf_op jit(solution)/shard_map/psum | solution.py:823
  494.3 3.7 copy-start.50
  497.9 63.3 %copy-start.47 = (f32[768]{0:T(1024)S(1)}, f32[768]{0:T(1024)}, u32[]{:S(2)}) copy-start(f32[768]{0:T(1024)} %param.19) | copy-start | bytes 9220
  604.7 84.4 %copy-start.1 = (bf16[192,768]{1,0:T(8,128)(2,1)S(1)}, bf16[192,768]{1,0:T(8,128)(2,1)}, u32[]{:S(2)}) copy-start(bf16[192,768]{1,0:T(8,128)(2,1)} %param.18) | copy-start | bytes 884740
  685.5 2.9 copy-start.45
  (17 other events, 17.5 us)
Sparse Core Ops, SparseCore 0:
  125.7 50.2 all-reduce.11
  224.9 47.7 all-reduce.13
  321.7 38.8 all-reduce.15
  362.9 105.2 all-reduce.17
  480.7 80.4 all-reduce.21
  565.2 120.2 all-reduce.19
Sparse Core Ops, SparseCore 1:
  128.1 42.3 all-gather.4
  172.4 40.0 all-gather.2
  487.9 67.9 reduce-scatter.2
  560.4 97.1 reduce-scatter.4
